TPU v7x, 512 devices: a whole 4x8x8 slice. The times are simulated.
512 devices in a mesh: row: 8 (over z_hi, core), col: 64 (over y, x, z_lo).
Axes of the slice: x: 4, y: 8, z: 8 (z_hi: 4, z_lo: 2; z = z_hi * 2 + z_lo), core: 2. Of those that a mesh axis runs over, the one named last changes fastest.
Arguments:
- matrix: float32 [8, 8, 256, 16384], P(None, 'row', None, 'col'), may hold values from -7.5 to 7.5, as said below
Outputs:
- reduced: float32 [8, 8, 256, 16384], P(None, 'row', None, 'col')
Inputs may be any that keep to these rules, and one draw needn't show every extreme that they name: The stored order-16384 matrix equals its transpose.
All inputs are finite; a program needn't handle non-finite values.
Results may differ from a plain program's by a relative error of at most 0.00015.
Values sent between devices are 32-bit elements; how exact they have to be, the bound alone decides.
A program may use at most 64 MiB of HBM per device.

v0:
```python
import jax
import jax.numpy as jnp
from jax import lax
from jax.sharding import PartitionSpec as P


def broadcast(shard, axis, root):
    mine = lax.axis_index(axis) == root
    return lax.psum(jnp.where(mine, shard, jnp.zeros_like(shard)), axis)


def exact_dot(left, right):
    return jnp.dot(left, right, precision=lax.Precision.HIGHEST, preferred_element_type=jnp.float32)


def exact_tdot(left, right):
    return lax.dot_general(
        left,
        right,
        (((0,), (0,)), ((), ())),
        precision=lax.Precision.HIGHEST,
        preferred_element_type=jnp.float32,
    )


def invert_square(target):
    identity = jnp.eye(target.shape[0], dtype=jnp.float32)
    normal_matrix = exact_tdot(target, target)
    factor = jnp.linalg.cholesky(normal_matrix)
    approx = jax.scipy.linalg.cho_solve((factor, True), target.T)
    for sweep_index in range(2):
        approx = exact_dot(approx, 2.0 * identity - exact_dot(target, approx))
    return approx


def on_device(matrix):
    row_count = lax.axis_size("row")
    row_index = lax.axis_index("row")
    col_index = lax.axis_index("col")
    row_blocks = matrix.shape[0]
    width = matrix.shape[2]
    local_rows = row_blocks * width
    current = matrix.reshape(local_rows, width)
    identity = jnp.eye(width, dtype=jnp.float32)
    global_block = jnp.arange(row_blocks, dtype=jnp.int32) * row_count + row_index
    live_flags = (global_block > 0)[:, None, None]
    first_flags = (global_block == 1)[:, None, None]
    panel_flags = (global_block == 0)[:, None, None]
    col_live = col_index > 0
    cur_three = current.reshape(row_blocks, width, width)
    panel_local = jnp.where(live_flags, cur_three, 0.0).reshape(local_rows, width)
    panel_here = broadcast(panel_local, "col", 0)
    gram_sum = lax.psum(exact_tdot(panel_here, panel_here), "row")
    lower = jnp.linalg.cholesky(gram_sum)
    lower_inv = jax.scipy.linalg.solve_triangular(lower, identity, lower=True)
    basis = exact_dot(panel_here, lower_inv.T)
    basis_three = basis.reshape(row_blocks, width, width)
    reflect_three = jnp.where(first_flags, identity[None], 0.0) - basis_three
    reflect_rows = reflect_three.reshape(local_rows, width)
    corner_piece = basis_three[1 // row_count]
    corner = broadcast(corner_piece, "row", 1 % row_count)
    kernel = invert_square(identity - corner.T)
    reflect_piece = lax.dynamic_index_in_dim(
        reflect_three, col_index // row_count, 0, keepdims=False
    )
    reflect_col = broadcast(reflect_piece, "row", col_index % row_count)
    reflect_col = jnp.where(col_live, reflect_col, 0.0)
    slab = current
    share = lax.psum_scatter(exact_dot(slab, reflect_col), "col", scatter_dimension=0, tiled=True)
    image_full = lax.all_gather(share, "col", axis=0, tiled=True)
    image_three = jnp.where(live_flags, image_full.reshape(row_blocks, width, width), 0.0)
    image_rows = image_three.reshape(local_rows, width)
    image_piece = lax.dynamic_index_in_dim(image_three, col_index // row_count, 0, keepdims=False)
    image_col = broadcast(image_piece, "row", col_index % row_count)
    image_col = jnp.where(col_live, image_col, 0.0)
    curvature = lax.psum(exact_tdot(reflect_col, image_col), "col")
    inner = exact_dot(exact_dot(kernel.T, curvature), kernel)
    left_factor = exact_dot(image_col, kernel) - 0.5 * exact_dot(reflect_col, inner + inner.T)
    right_factor = exact_dot(reflect_col, kernel.T)
    update = exact_dot(reflect_rows, left_factor.T) + exact_dot(image_rows, right_factor.T)
    update_three = update.reshape(row_blocks, width, width)
    band_rows = jnp.where(first_flags, lower.T[None], 0.0)
    band_cols = jnp.where(col_index == 1, lower, 0.0)[None]
    result_three = jnp.where(live_flags & col_live, cur_three - update_three, cur_three)
    result_three = jnp.where(live_flags & (col_index == 0), band_rows, result_three)
    result_three = jnp.where(panel_flags & col_live, band_cols, result_three)
    current = result_three.reshape(local_rows, width)
    return current.reshape(matrix.shape)


def solution(mesh):
    return jax.shard_map(
        on_device,
        mesh=mesh,
        in_specs=(P(None, "row", None, "col"),),
        out_specs=P(None, "row", None, "col"),
        check_vma=False,
    )
```

profile of v0, /device:TPU:1, one launch (start us, length us, event | category | flops | bytes accessed | tf_op | source)
XLA Modules:
  0.0 2181.1 jit_solution(11676806572987849326)
XLA Ops:
  6.6 2.8 select_select_fusion
  9.5 580.0 %all-reduce.8.cloned.1.call-done = f32[2048,256]{1,0:T(8,128)} async-done(((f32[2048,256]{1,0:T(8,128)}), f32[2048,256]{1,0:T(8,128)}) %all-reduce.8.cloned.1.call-update) | async-done | bytes 2097168 | tf_op jit(solution)/shard_map/psum | solution.py:9
  589.5 6.4 fusion.70
  596.8 117.9 %all-reduce.10.cloned.1.call-done = f32[256,256]{0,1:T(8,128)} async-done(((f32[256,256]{0,1:T(8,128)}), f32[256,256]{0,1:T(8,128)}) %all-reduce.10.cloned.1.call-update) | async-done | bytes 262160 | tf_op jit(solution)/shard_map/psum | solution.py:53
  716.9 11.7 cholesky.130
  728.6 9.8 custom-call.18
  738.9 11.7 cholesky.147
  752.8 4.1 while.6
  753.6 1.3 bitcast_dynamic-update-slice_fusion.5
  755.5 1.3 bitcast_dynamic-update-slice_fusion.5
  756.9 19.7 custom-call.19
  777.5 4.9 fusion.2
  785.1 76.6 %all-reduce.12.cloned.1.call-done = f32[256,256]{1,0:T(8,128)} async-done(((f32[256,256]{1,0:T(8,128)}), f32[256,256]{1,0:T(8,128)}) %all-reduce.12.cloned.1.call-update) | async-done | bytes 262160 | tf_op jit(solution)/shard_map/psum | solution.py:9
  861.7 3.2 convolution_bitcast_fusion
  864.9 271.0 %reduce-scatter.2.cloned.1.call-done = f32[32,256]{1,0:T(8,128)} async-done(((f32[2048,256]{1,0:T(8,128)}), f32[32,256]{1,0:T(8,128)}) %reduce-scatter.2.cloned.1.call-update) | async-done | bytes 32784 | tf_op jit(solution)/shard_map/reduce_scatter | solution.py:69
  1138.5 302.4 %all-gather.2.cloned.1.call-done = f32[2048,256]{1,0:T(8,128)} async-done(((f32[32,256]{1,0:T(8,128)}), f32[2048,256]{1,0:T(8,128)}) %all-gather.2.cloned.1.call-update) | async-done | bytes 2097168 | tf_op jit(solution)/shard_map/all_gather | solution.py:70
  1440.9 2.4 fusion.8
  1444.4 120.1 %all-reduce.16.cloned.1.call-done = (f32[256,256]{0,1:T(8,128)}, f32[256,256]{1,0:T(8,128)}) async-done(((f32[256,256]{0,1:T(8,128)}, f32[256,256]{1,0:T(8,128)}), (f32[256,256]{0,1:T(8,128)}, f32[256,256]{1,0:T(8,128)})) %all-reduce.16.cloned.1.call-update) | async-done | bytes 524304 | tf_op jit(solution)/shard_map/psum | solution.py:9
  1564.5 1.7 convert_subtract_fusion
  1566.2 1.6 fusion.45
  1568.0 11.7 cholesky.164
  1580.4 9.8 custom-call.20
  1590.8 11.7 cholesky.181
  1604.4 4.1 while.5
  1608.6 19.7 custom-call.15
  1633.6 1.3 fusion.19
  1637.2 525.6 %all-reduce.14.cloned.1.call-done = f32[256,256]{1,0:T(8,128)} async-done(((f32[256,256]{1,0:T(8,128)}), f32[256,256]{1,0:T(8,128)}) %all-reduce.14.cloned.1.call-update) | async-done | bytes 262160 | tf_op jit(solution)/shard_map/psum | solution.py:76
  2162.7 1.5 fusion.72
  2164.8 1.4 fusion.4
  2166.2 3.7 fusion.74
  2169.9 2.1 convolution_add_fusion
  2172.1 2.0 fusion.1
  (98 shorter events, 27.0 us)
Async XLA Ops:
  6.5 582.9 %all-reduce.8.cloned.1.call-start = ((), (), s32[]{:S(2)}) async-start(), calls=%async_computation.1 | async-start | bytes 4194304 | tf_op jit(solution)/shard_map/psum | solution.py:9
  9.4 705.3 %all-reduce.10.cloned.1.call-start = ((), (), s32[]{:S(2)}) async-start(), calls=%async_computation.2 | async-start | bytes 524288 | tf_op jit(solution)/shard_map/psum | solution.py:53
  595.9 265.8 %all-reduce.12.cloned.1.call-start = ((), (), s32[]{:S(2)}) async-start(), calls=%async_computation.3 | async-start | bytes 524288 | tf_op jit(solution)/shard_map/psum | solution.py:9
  777.5 84.2 %copy-start = (f32[8,1,256,256]{3,2,1,0:T(8,128)S(1)}, f32[8,1,256,256]{3,2,1,0:T(8,128)}, u32[]{:S(2)}) copy-start(f32[8,1,256,256]{3,2,1,0:T(8,128)} %param.4) | copy-start | bytes 6291460
  782.4 1.3 copy-start.3
  785.0 350.9 %reduce-scatter.2.cloned.1.call-start = ((), (), s32[]{:S(2)}) async-start(), calls=%async_computation.4 | async-start | bytes 2129920 | tf_op jit(solution)/shard_map/reduce_scatter | solution.py:69
  864.9 576.0 %all-gather.2.cloned.1.call-start = ((), (), s32[]{:S(2)}) async-start(), calls=%async_computation.5 | async-start | bytes 2129920 | tf_op jit(solution)/shard_map/all_gather | solution.py:70
  1136.0 428.5 %all-reduce.16.cloned.1.call-start = ((), (), s32[]{:S(2)}) async-start(), calls=%async_computation.7 | async-start | bytes 1048576 | tf_op jit(solution)/shard_map/psum | solution.py:9
  1443.3 719.4 %all-reduce.14.cloned.1.call-start = ((), (), s32[]{:S(2)}) async-start(), calls=%async_computation.6 | async-start | bytes 524288 | tf_op jit(solution)/shard_map/psum | solution.py:76
  1590.5 41.5 %copy-start.1 = (f32[256,256]{0,1:T(8,128)S(1)}, f32[256,256]{0,1:T(8,128)}, u32[]{:S(2)}) copy-start(f32[256,256]{0,1:T(8,128)} %get-tuple-element.47) | copy-start | bytes 786436
  1631.1 2.5 copy-start.2
  1631.1 2.5 copy-start.6
  2166.2 3.7 copy-start.4
  2166.2 3.7 copy-start.5
  2169.9 2.2 copy-start.7
Sparse Core Ops, SparseCore 0:
  10.3 579.1 all-reduce.7
  596.0 118.7 all-reduce.9
  785.1 76.5 all-reduce.11
  865.0 270.8 reduce-scatter.1
  1137.9 302.9 all-gather.1
  1443.7 120.7 all-reduce.15
  1635.1 527.6 all-reduce.13
where the time goes:
time: 2210 us; the launch traced here: 2180 us
  waiting for transfers between devices  1990 us (90%)
  other arithmetic  121 us (5%)
  matrix products  35.7 us (2%)
    psum x3, waiting for transfers between devices, broadcast(): return lax.psum(jnp.where(mine, shard, jnp.zeros_like(shard)), axis)  777 us
    psum x1, waiting for transfers between devices, on_device(): curvature = lax.psum(exact_tdot(reflect_col, image_col), 'col')  526 us
    all_gather x1, waiting for transfers between devices, on_device(): image_full = lax.all_gather(share, 'col', axis=0, tiled=True)  302 us
    reduce_scatter x1, waiting for transfers between devices, on_device(): lax.psum_scatter(exact_dot(slab, reflect_col), 'col', scatter_dimension=0...  271 us
    psum x1, waiting for transfers between devices, on_device(): gram_sum = lax.psum(exact_tdot(panel_here, panel_here), 'row')  118 us
  transfers between devices with their start and end apart: 7, of which 7 were waited for; matrix products, arithmetic and copies ran while one was open for 0% of the time, Pallas kernels for 0%

commit v1 on v0

v1 whole, which is shorter than its diff:
```python
import functools

import jax
import jax.numpy as jnp
from jax import lax
from jax.experimental import pallas as pl
from jax.experimental.pallas import tpu as pltpu
from jax.sharding import PartitionSpec as P

NY, NX, NZ, NL, NC = 8, 4, 4, 2, 2
W = 256
SUB = 32
QR = W // 4
F32, BF16 = jnp.float32, jnp.bfloat16
MESH = pl.DeviceIdType.MESH
VMEM_LIMIT = 48 * 1024 * 1024
NN = (((1,), (0,)), ((), ()))
NT = (((1,), (1,)), ((), ()))
TN = (((0,), (0,)), ((), ()))


def split2(v):
    hi = v.astype(BF16)
    return hi, (v - hi.astype(F32)).astype(BF16)


def split3(v):
    a = v.astype(BF16)
    rest = v - a.astype(F32)
    b = rest.astype(BF16)
    return a, b, (rest - b.astype(F32)).astype(BF16)


def mm(a, b, dims):
    return lax.dot_general(a, b, dims, preferred_element_type=F32)


def dot3(a, b, dims=NN):
    ah, al = split2(a)
    bh, bl = split2(b)
    return mm(ah, bh, dims) + (mm(ah, bl, dims) + mm(al, bh, dims))


def dot6(a, b, dims=NN):
    a1, a2, a3 = split3(a)
    b1, b2, b3 = split3(b)
    low = mm(a2, b2, dims) + (mm(a1, b3, dims) + mm(a3, b1, dims))
    return mm(a1, b1, dims) + ((mm(a1, b2, dims) + mm(a2, b1, dims)) + low)


def packed_tdot(a, b):
    a1, a2, a3 = split3(a)
    b1, b2, b3 = split3(b)
    left = jnp.concatenate([a1, a1, a2, a2, a1, a3], axis=0)
    right = jnp.concatenate([b1, b2, b1, b2, b3, b1], axis=0)
    return mm(left, right, TN)


def iota(shape, dim):
    return lax.broadcasted_iota(jnp.int32, shape, dim)


class Place:
    def __init__(self):
        self.r = lax.axis_index("row")
        self.c = lax.axis_index("col")
        self.z, self.h = self.r // NC, self.r % NC
        self.y, self.x, self.l = self.c // (NX * NL), (self.c // NL) % NX, self.c % NL
        self.piece = self.h * NZ + self.z
        self.native = self.l == self.h
        self.diag = jnp.logical_and(self.native, self.x == self.z)

    def at_y(self, d):
        return (self.r, ((self.y + d) % NY * NX + self.x) * NL + self.l)

    def at_x(self, d):
        return (self.r, (self.y * NX + (self.x + d) % NX) * NL + self.l)

    def at_l(self):
        return (self.r, (self.y * NX + self.x) * NL + (1 - self.l))

    def at_z(self, d):
        return (((self.z + d) % NZ) * NC + self.h, self.c)

    def at_core(self):
        return (self.z * NC + (1 - self.h), self.c)

    def at_row(self, d):
        return ((self.r + d) % (NZ * NC), self.c)


def rcopy(src, dst, send, recv, device):
    return pltpu.make_async_remote_copy(
        src_ref=src, dst_ref=dst, send_sem=send, recv_sem=recv, device_id=device, device_id_type=MESH
    )


def greet(devices):
    barrier = pltpu.get_barrier_semaphore()
    for device in devices:
        pl.semaphore_signal(barrier, inc=1, device_id=device, device_id_type=MESH)
    pl.semaphore_wait(barrier, len(devices))


def loop(n, body):
    def step(t, carry):
        body(t)
        return carry

    lax.fori_loop(0, n, step, 0)


class Spread:
    def __init__(self, place, buf, recv, send_x, send_y, send_l):
        self.p, self.buf, self.recv = place, buf, recv
        self.send_x, self.send_y, self.send_l = send_x, send_y, send_l

    def chunk(self, i, q):
        return self.buf.at[i, pl.ds(pl.multiple_of(q * QR, QR), QR)]

    def copy(self, i, q, send, device):
        part = self.chunk(i, q)
        return rcopy(part, part, send, self.recv.at[i, q], device)

    def to_x(self, d, q):
        return self.copy(self.p.y, q, self.send_x.at[d - 1, q], self.p.at_x(d))

    def to_y(self, side, s, q):
        sign = 1 if side == 0 else -1
        i = (self.p.y - sign * s + NY) % NY
        return self.copy(i, q, self.send_y.at[side, s, q], self.p.at_y(sign + NY))

    def to_l(self, i, q):
        return self.copy(i, q, self.send_l.at[i, q], self.p.at_l())

    def arrive(self, i, q):
        self.copy(i, q, self.send_l.at[i, q], self.p.at_l()).wait_recv()

    def own(self, home):
        p = self.p

        def body(q):
            @pl.when(jnp.logical_and(p.native, jnp.logical_not(home)))
            def _():
                self.arrive(p.y, q)

            @pl.when(jnp.logical_and(jnp.logical_not(p.native), q < 2))
            def _():
                self.arrive(p.y, q)

            @pl.when(p.diag)
            def _():
                for d in (1, 3, 2):
                    self.to_x(d, q).start()

            @pl.when(p.native)
            def _():
                self.to_l(p.y, q).start()

            @pl.when(jnp.logical_or(p.native, q < 2))
            def _():
                self.to_y(0, 0, q).start()
                self.to_y(1, 0, q).start()

        loop(4, body)

    def sends_y(self, side, s, q):
        if s < 3:
            return jnp.logical_or(self.p.native, q < 2)
        if side == 0:
            return q < jnp.where(self.p.native, 2, 1)
        return jnp.where(self.p.native, q // 2 == 1, q == 1)

    def ring(self, s):
        p = self.p
        for side in (0, 1):
            sign = 1 if side == 0 else -1
            i = (p.y - sign * s + NY) % NY

            def body(q, side=side, i=i):
                @pl.when(jnp.logical_or(p.native, q < 2))
                def _():
                    self.arrive(i, q)

                @pl.when(self.sends_y(side, s, q))
                def _():
                    self.to_y(side, s, q).start()

                @pl.when(jnp.logical_and(p.native, q >= 2))
                def _():
                    self.to_l(i, q).start()

            loop(4, body)

    def last(self):
        p = self.p
        i = (p.y + 4) % NY

        def body(q):
            @pl.when(jnp.logical_or(p.native, q < 2))
            def _():
                self.arrive(i, q)

            @pl.when(jnp.logical_and(p.native, q >= 2))
            def _():
                self.to_l(i, q).start()

        loop(4, body)

        @pl.when(jnp.logical_not(p.native))
        def _():
            def late(t):
                self.arrive(t // 2, 2 + t % 2)

            loop(2 * NY, late)

    def drain(self):
        p = self.p

        def body(q):
            @pl.when(p.diag)
            def _():
                for d in (1, 2, 3):
                    self.to_x(d, q).wait_send()

            for s in range(4):
                for side in (0, 1):

                    @pl.when(self.sends_y(side, s, q))
                    def _(s=s, side=side):
                        self.to_y(side, s, q).wait_send()

            @pl.when(p.native)
            def _():
                self.to_l(p.y, q).wait_send()

            @pl.when(jnp.logical_and(p.native, q >= 2))
            def _():
                def others(t):
                    self.to_l((p.y + 1 + t) % NY, q).wait_send()

                loop(NY - 1, others)

        loop(4, body)


SPREAD_SEMS = [
    pltpu.SemaphoreType.DMA((NY, 4)),
    pltpu.SemaphoreType.DMA((3, 4)),
    pltpu.SemaphoreType.DMA((2, 4, 4)),
    pltpu.SemaphoreType.DMA((NY, 4)),
]


class RowGather:
    def __init__(self, place, buf, lo, hi, recv, send):
        self.p, self.buf, self.lo, self.hi = place, buf, lo, hi
        self.recv, self.send = recv, send

    def copy(self, j, slot, device):
        part = self.buf.at[pl.ds(self.lo, self.hi - self.lo), j]
        return rcopy(part, part, self.send.at[slot], self.recv.at[j], device)

    def to_z(self, d):
        return self.copy(self.p.piece, d - 1, self.p.at_z(d))

    def to_core(self, d):
        j = self.p.h * NZ + (self.p.z - d + NZ) % NZ
        return self.copy(j, 3 + d, self.p.at_core())

    def start(self):
        for d in (1, 3, 2):
            self.to_z(d).start()
        self.to_core(0).start()

    def relay(self):
        for d in (1, 3, 2):
            self.to_core(d).wait_recv()
            self.to_core(d).start()

    def finish(self):
        for d in range(4):
            j = (1 - self.p.h) * NZ + (self.p.z - d + NZ) % NZ
            self.copy(j, 3 + d, self.p.at_core()).wait_recv()
        for d in (1, 2, 3):
            self.to_z(d).wait_send()
        for d in range(4):
            self.to_core(d).wait_send()


GATHER_SEMS = [pltpu.SemaphoreType.DMA((NZ * NC,)), pltpu.SemaphoreType.DMA((7,))]


def row_piece(r):
    return (r % NC) * NZ + r // NC


class RowScatter:
    def __init__(self, place, root, src, dst, recv, send):
        self.p, self.root, self.src, self.dst = place, root, src, dst
        self.recv, self.send = recv, send

    def copy(self, d):
        j = row_piece((self.p.r + d) % (NZ * NC))
        part = self.src.at[pl.ds(pl.multiple_of(j * SUB, SUB), SUB)]
        return rcopy(part, self.dst.at[j], self.send.at[d - 1], self.recv, self.p.at_row(d))

    def start(self):
        @pl.when(self.p.r == self.root)
        def _():
            for d in range(1, 8):
                self.copy(d).start()
            self.dst[self.p.piece] = self.src[pl.ds(pl.multiple_of(self.p.piece * SUB, SUB), SUB)]

    def arrive(self):
        @pl.when(self.p.r != self.root)
        def _():
            self.copy(1).wait_recv()

    def finish(self):
        @pl.when(self.p.r == self.root)
        def _():
            for d in range(1, 8):
                self.copy(d).wait_send()


SCATTER_SEMS = [pltpu.SemaphoreType.DMA(()), pltpu.SemaphoreType.DMA((7,))]

GRAM, PROD, FIRST, PANEL, NEXT = range(5)


def gather_kernel(a_ref, prow, agb, src, part, rb_core, sums, rb_z, *sems):
    sp_sems, ge, gl, sc3, sc4, sc2, zs, ar = (
        sems[0:4], sems[4:6], sems[6:8], sems[8:10], sems[10:12], sems[12:14], sems[14], sems[15:19])
    p = Place()
    greet([p.at_row(d) for d in range(1, 8)] + [p.at_y(1), p.at_y(NY - 1), p.at_l()]
          + [p.at_x(d) for d in (1, 2, 3)])

    spread = Spread(p, prow, *sp_sems)
    home_row = p.x * NC + p.l
    home = jnp.logical_and(p.diag, p.r == 0)

    @pl.when(p.r == 0)
    def _():
        src[...] = jnp.where(p.c == 0, 0.0, a_ref[0])

    @pl.when(p.r == 1)
    def _():
        src[...] = a_ref[0]

    def to_home(q):
        rows = pl.ds(pl.multiple_of(q * QR, QR), QR)
        return rcopy(src.at[rows], prow.at[p.y, rows], zs.at[q], sp_sems[0].at[p.y, q], (home_row, p.c))

    @pl.when(home)
    def _():
        prow[p.y] = src[...]

    sends_home = jnp.logical_and(p.r == 0, home_row != 0)

    @pl.when(sends_home)
    def _():
        loop(4, lambda q: to_home(q).start())

    panel = RowScatter(p, 0, src, agb.at[PANEL], *sc3)
    following = RowScatter(p, 1, src, agb.at[NEXT], *sc4)
    panel.start()
    following.start()

    spread.own(home)
    panel.arrive()
    following.arrive()
    early = RowGather(p, agb, PANEL, NEXT + 1, *ge)
    early.start()
    spread.ring(1)
    spread.ring(2)
    early.relay()
    spread.ring(3)
    spread.last()

    first = RowScatter(p, 1, prow.at[0], agb.at[FIRST], *sc2)
    first.start()

    part[...] = jnp.zeros_like(part)

    def products(i):
        block = prow[i]
        bh, bl = split2(block)
        ah, al = split2(a_ref[i])
        gram = mm(bh, bh, NT) + (mm(bh, bl, NT) + mm(bl, bh, NT))
        prod = mm(bh, ah, NN) + (mm(bh, al, NN) + mm(bl, ah, NN))
        part[GRAM] += gram.reshape(8, SUB, W)
        part[PROD] += prod.reshape(8, SUB, W)

    loop(NY, products)

    send_c, recv_c, send_z, recv_z = ar
    out = rcopy(part.at[:, pl.ds(pl.multiple_of((1 - p.h) * NZ, NZ), NZ)], rb_core, send_c, recv_c, p.at_core())
    out.start()
    out.wait_recv()
    sums[...] = part[:, pl.ds(pl.multiple_of(p.h * NZ, NZ), NZ)] + rb_core[...]

    def to_z(d):
        return rcopy(sums.at[:, (p.z + d) % NZ], rb_z.at[d - 1], send_z.at[d - 1], recv_z.at[d - 1], p.at_z(d))

    for d in (1, 3, 2):
        to_z(d).start()
    total = sums[:, p.z]
    for d in (1, 3, 2):
        to_z(d).wait_recv()
        total = total + rb_z[d - 1]
    agb[GRAM, p.piece] = total[0]
    agb[PROD, p.piece] = total[1]
    first.arrive()
    late = RowGather(p, agb, GRAM, FIRST + 1, *gl)
    late.start()
    early.finish()
    late.relay()
    late.finish()

    out.wait_send()
    for d in (1, 2, 3):
        to_z(d).wait_send()
    for each in (panel, following, first):
        each.finish()

    @pl.when(sends_home)
    def _():
        loop(4, lambda q: to_home(q).wait_send())

    spread.drain()


def gather_call(slab):
    whole = pl.BlockSpec(memory_space=pltpu.VMEM)
    return pl.pallas_call(
        gather_kernel,
        out_shape=(jax.ShapeDtypeStruct((NY, W, W), F32), jax.ShapeDtypeStruct((5, 8, SUB, W), F32)),
        in_specs=[whole],
        out_specs=(whole, whole),
        scratch_shapes=[
            pltpu.VMEM((W, W), F32),
            pltpu.VMEM((2, 8, SUB, W), F32),
            pltpu.VMEM((2, NZ, SUB, W), F32),
            pltpu.VMEM((2, NZ, SUB, W), F32),
            pltpu.VMEM((3, 2, SUB, W), F32),
        ]
        + SPREAD_SEMS + GATHER_SEMS + GATHER_SEMS + SCATTER_SEMS * 3
        + [pltpu.SemaphoreType.DMA((4,))]
        + [pltpu.SemaphoreType.DMA(()), pltpu.SemaphoreType.DMA(()),
           pltpu.SemaphoreType.DMA((3,)), pltpu.SemaphoreType.DMA((3,))],
        compiler_params=pltpu.CompilerParams(
            collective_id=0, has_side_effects=True, vmem_limit_bytes=VMEM_LIMIT),
        name="gather_panel",
    )(slab)


def factor_steps(state, j):
    j0 = j * SUB
    rows = iota((SUB, 1), 0)
    panel = state["s"][j0:j0 + SUB, :]
    for t in range(SUB):
        col = panel[:, j0 + t:j0 + t + 1]
        inv = 1.0 / col[t:t + 1, :]
        factor = jnp.where(rows > t, col, 0.0)
        panel = panel - factor * (panel[t:t + 1, :] * inv)
        yield
    lanes = iota((SUB, W), 1)
    diag = jnp.sum(jnp.where(lanes == j0 + iota((SUB, W), 0), panel[:, :W], 0.0), axis=1, keepdims=True)
    panel = panel * (1.0 / jnp.sqrt(diag))
    upper = jnp.where(lanes >= j0 + iota((SUB, W), 0), panel[:, :W], 0.0)
    state["row"] = upper
    state["lt"][j0:j0 + SUB, :] = upper
    state["y"][j0:j0 + SUB, :] = panel[:, W:]
    if j < 7:
        whole = jnp.concatenate([upper, panel[:, W:]], axis=1)
        state["s"][j0 + SUB:, :] -= packed_tdot(upper[:, j0 + SUB:] if (j0 + SUB) % 128 == 0 else upper, whole)[
            (0 if (j0 + SUB) % 128 == 0 else j0 + SUB):, :]


def invert_steps(m_ref, row, j):
    j0 = j * SUB
    cols = slice(j0, j0 + SUB)
    m_ref[:, cols] += row.T
    lanes = iota((SUB, W), 1)
    rows = iota((SUB, W), 0)
    panel = m_ref[cols, :]
    for t in range(SUB):
        here = lanes == j0 + t
        col = panel[:, j0 + t:j0 + t + 1]
        inv = 1.0 / col[t:t + 1, :]
        pivot = jnp.where(here[t:t + 1, :], 1.0, panel[t:t + 1, :]) * inv
        panel = jnp.where(rows == t, pivot, jnp.where(here, 0.0, panel) - col * pivot)
        yield
    left = m_ref[:, cols].T
    keep = jnp.logical_and(iota((W, W), 1) >= j0, iota((W, W), 1) < j0 + SUB)
    m_ref[...] = jnp.where(keep, 0.0, m_ref[...]) - packed_tdot(left, panel)
    m_ref[cols, :] = panel


def solve_kernel(agb, lt, y_ref, k_ref, vt_ref, it_ref, image_ref, r_ref, curv_ref, s, m):
    p = Place()
    eye = (iota((W, W), 0) == iota((W, W), 1)).astype(F32)
    s[:, :W] = agb[GRAM].reshape(W, W)
    s[:, W:] = eye
    m[...] = -agb[FIRST].reshape(W, W)
    state = dict(s=s, lt=lt, y=y_ref)
    previous = None
    for j in range(9):
        ahead = factor_steps(state, j) if j < 8 else iter(())
        behind = invert_steps(m, previous, j - 1) if j > 0 else iter(())
        running = [behind, ahead]
        while running:
            for each in list(running):
                if next(each, running) is running:
                    running.remove(each)
        previous = state["row"]
    chol_t, inv, near = lt[...], y_ref[...], m[...]
    panel = agb[PANEL].reshape(W, W)
    shifted = jnp.where(p.c == 1, chol_t.T, 0.0) - panel
    vt = dot6(inv, shifted)
    it = agb[NEXT].reshape(W, W) - dot6(inv, agb[PROD].reshape(W, W))
    k_ref[...] = dot6(near, chol_t, NT)
    r_ref[...] = dot6(near, shifted)
    vt_ref[...] = vt
    it_ref[...] = it
    image_ref[...] = it.T
    mine = vt_ref[pl.ds(pl.multiple_of(p.piece * SUB, SUB), SUB), :]
    curv_ref[...] = dot6(mine, it, NT)


def solve_call(agb):
    whole = pl.BlockSpec(memory_space=pltpu.VMEM)
    square = jax.ShapeDtypeStruct((W, W), F32)
    return pl.pallas_call(
        solve_kernel,
        out_shape=(square,) * 7 + (jax.ShapeDtypeStruct((SUB, W), F32),),
        in_specs=[whole],
        out_specs=(whole,) * 8,
        scratch_shapes=[pltpu.VMEM((W, 2 * W), F32), pltpu.VMEM((W, W), F32)],
        compiler_params=pltpu.CompilerParams(vmem_limit_bytes=VMEM_LIMIT),
        name="solve_small",
    )(agb)


def image_kernel(image, curv, irow, cgather, s1, rb1, rb2, s2, rb3, s3, rb4, *sems):
    sp_sems, ge, c1, c2, c3, c4 = sems[0:4], sems[4:6], sems[6:8], sems[8:10], sems[10:12], sems[12:14]
    p = Place()
    greet([p.at_row(d) for d in range(1, 8)] + [p.at_y(d) for d in range(1, 8)] + [p.at_l()]
          + [p.at_x(d) for d in (1, 2, 3)])
    spread = Spread(p, irow, *sp_sems)

    @pl.when(p.diag)
    def _():
        irow[p.y] = image[...]

    def to_l():
        return rcopy(curv, rb1, c1[0], c1[1], p.at_l())

    def to_x(d):
        x = (p.x + d) % NX
        return rcopy(s1.at[pl.ds(pl.multiple_of(x * 8, 8), 8)], rb2.at[d - 1], c2[0].at[d - 1], c2[1].at[d - 1], p.at_x(d))

    def to_y(d):
        return rcopy(s2, rb3.at[d - 1], c3[0].at[d - 1], c3[1].at[d - 1], p.at_y(d))

    def back_x(d):
        rows = pl.ds(pl.multiple_of(p.x * 8, 8), 8)
        return rcopy(s3, rb4.at[rows], c4[0].at[d - 1], c4[1].at[d - 1], p.at_x(d))

    to_l().start()
    spread.own(p.diag)
    to_l().wait_recv()
    s1[...] = curv[...] + rb1[...]
    for d in (1, 2, 3):
        to_x(d).start()
    spread.ring(1)
    total = s1[pl.ds(pl.multiple_of(p.x * 8, 8), 8)]
    for d in (1, 2, 3):
        to_x(d).wait_recv()
        total = total + rb2[d - 1]
    s2[...] = total
    for d in range(1, 8):
        to_y(d).start()
    spread.ring(2)
    total = s2[...]
    for d in range(1, 8):
        to_y(d).wait_recv()
        total = total + rb3[d - 1]
    s3[...] = total
    for d in (1, 2, 3):
        back_x(d).start()
    rb4[pl.ds(pl.multiple_of(p.x * 8, 8), 8)] = total
    spread.ring(3)
    for d in (1, 2, 3):
        back_x(d).wait_recv()
    cgather[0, p.piece] = rb4[...]
    gather = RowGather(p, cgather, 0, 1, *ge)
    gather.start()
    spread.last()
    gather.relay()
    gather.finish()
    to_l().wait_send()
    for d in (1, 2, 3):
        to_x(d).wait_send()
        back_x(d).wait_send()
    for d in range(1, 8):
        to_y(d).wait_send()
    spread.drain()


def image_call(image, curv):
    whole = pl.BlockSpec(memory_space=pltpu.VMEM)
    dma = pltpu.SemaphoreType.DMA
    return pl.pallas_call(
        image_kernel,
        out_shape=(jax.ShapeDtypeStruct((NY, W, W), F32), jax.ShapeDtypeStruct((1, 8, SUB, W), F32)),
        in_specs=[whole, whole],
        out_specs=(whole, whole),
        scratch_shapes=[
            pltpu.VMEM((SUB, W), F32),
            pltpu.VMEM((SUB, W), F32),
            pltpu.VMEM((3, 8, W), F32),
            pltpu.VMEM((8, W), F32),
            pltpu.VMEM((7, 8, W), F32),
            pltpu.VMEM((8, W), F32),
            pltpu.VMEM((SUB, W), F32),
        ]
        + SPREAD_SEMS + GATHER_SEMS
        + [dma(()), dma(()), dma((3,)), dma((3,)), dma((7,)), dma((7,)), dma((3,)), dma((3,))],
        compiler_params=pltpu.CompilerParams(
            collective_id=1, has_side_effects=True, vmem_limit_bytes=VMEM_LIMIT),
        name="spread_image",
    )(image, curv)


def update_kernel(a_ref, prow, irow, lt, y_ref, k_ref, vt_ref, it_ref, r_ref, curv, out, s_ref, u_ref, rn_ref):
    p = Place()
    i = pl.program_id(0)

    @pl.when(i == 0)
    def _():
        kern = k_ref[...]
        inner = dot3(dot3(kern, curv[0].reshape(W, W), TN), kern)
        s = dot3(kern, it_ref[...], TN) - 0.5 * dot3(inner + inner.T, vt_ref[...])
        s_ref[...] = s
        uh, ul = split2(dot3(y_ref[...], s, TN))
        u_ref[0] = uh
        u_ref[1] = ul
        rh, rl = split2(r_ref[...])
        rn_ref[0] = rh
        rn_ref[1] = rl

    ph, plo = split2(prow[0])
    ih, il = split2(irow[0])
    first = mm(ph, u_ref[0], TN) + (mm(ph, u_ref[1], TN) + mm(plo, u_ref[0], TN))
    second = mm(ih, rn_ref[0], NN) + (mm(ih, rn_ref[1], NN) + mm(il, rn_ref[0], NN))
    b = i * (NZ * NC) + p.r
    res = a_ref[0] + (first - second)
    res = jnp.where(b == 1, res - s_ref[...], res)
    out[0] = res

    @pl.when(p.c == 0)
    def _():
        out[0] = jnp.where(b == 0, a_ref[0], jnp.where(b == 1, lt[...], 0.0))

    @pl.when(jnp.logical_and(p.c > 0, b == 0))
    def _():
        out[0] = jnp.where(p.c == 1, lt[...].T, 0.0)


def update_call(slab, prow, irow, lt, y, k, vt, it, r, curv):
    tile = pl.BlockSpec((1, W, W), lambda i: (i, 0, 0))
    square = pl.BlockSpec((W, W), lambda i: (0, 0))
    return pl.pallas_call(
        update_kernel,
        grid=(NY,),
        out_shape=jax.ShapeDtypeStruct((NY, W, W), F32),
        in_specs=[tile, tile, tile] + [square] * 6 + [pl.BlockSpec((1, 8, SUB, W), lambda i: (0, 0, 0, 0))],
        out_specs=tile,
        scratch_shapes=[pltpu.VMEM((W, W), F32), pltpu.VMEM((2, W, W), BF16), pltpu.VMEM((2, W, W), BF16)],
        compiler_params=pltpu.CompilerParams(vmem_limit_bytes=VMEM_LIMIT),
        name="update_rows",
    )(slab, prow, irow, lt, y, k, vt, it, r, curv)


def on_device(matrix):
    slab = matrix.reshape(NY, W, W)
    prow, agb = gather_call(slab)
    lt, y, k, vt, it, image, r, curv = solve_call(agb)
    irow, cgather = image_call(image, curv)
    out = update_call(slab, prow, irow, lt, y, k, vt, it, r, cgather)
    return out.reshape(matrix.shape)


def solution(mesh):
    return jax.shard_map(
        on_device,
        mesh=mesh,
        in_specs=(P(None, "row", None, "col"),),
        out_specs=P(None, "row", None, "col"),
        check_vma=False,
    )
```

time: 2210 us -> 160 us (0.07); the launches traced: 2180 us -> 160 us
  waiting for transfers between devices: 1990 us -> 0 us
  Pallas kernels: 0 us -> 157 us
  other arithmetic: 121 us -> 0 us
  matrix products: 35.7 us -> 0 us
    psum x5 -> x0, waiting for transfers between devices: 1420 us -> none  [the longest x3 777 us: broadcast(): return lax.psum(jnp.where(mine, shard, jnp.zeros_like(shard)), axis)]
    all_gather x1 -> x0, waiting for transfers between devices: 302 us -> none  [on_device(): image_full = lax.all_gather(share, 'col', axis=0, tiled=True)]
    reduce_scatter x1 -> x0, waiting for transfers between devices: 271 us -> none  [on_device(): lax.psum_scatter(exact_dot(slab, reflect_col), 'col', scatter_dimension=0...]
    pallas_call x0 -> x4, Pallas kernels: none -> 157 us  [the longest x1 74.9 us: gather_call(): pl.pallas_call(gather_kernel, out_shape=(jax.ShapeDtypeStruct((NY, W, W),...]
    another operation x17 -> x0, other arithmetic: 108 us -> none  [the longest x7 34.6 us: invert_square(): factor = jnp.linalg.cholesky(normal_matrix)]
    dot_general x16 -> x0, matrix products: 30.3 us -> none  [the longest x13 20.9 us: exact_dot(): jnp.dot(left, right, precision=lax.Precision.HIGHEST, preferred_element_t...]
  transfers between devices with their start and end apart: 7 -> 0, of which waited for: 7 -> 0; matrix products, arithmetic and copies ran while one was open for 0% -> 0% of each run, Pallas kernels for 0% -> 0%
where the time goes in v1:
time: 160 us
  Pallas kernels  157 us (98%)
  local copies, waits for them, and re-layouts  2.93 us (2%)
    pallas_call x1, Pallas kernels, gather_call(): pl.pallas_call(gather_kernel, out_shape=(jax.ShapeDtypeStruct((NY, W, W),...  74.9 us
    pallas_call x1, Pallas kernels, image_call(): pl.pallas_call(image_kernel, out_shape=(jax.ShapeDtypeStruct((NY, W, W),...  43.7 us
    pallas_call x1, Pallas kernels, solve_call(): pl.pallas_call(solve_kernel, out_shape=(square,) * 7 + (jax.ShapeDtypeStr...  29.8 us
    pallas_call x1, Pallas kernels, update_call(): pl.pallas_call(update_kernel, grid=(NY,), out_shape=jax.ShapeDtypeStruct(...  8.45 us

profile of v1, /device:TPU:1, one launch (start us, length us, event | category | flops | bytes accessed | tf_op | source)
XLA Modules:
  0.0 159.8 jit_solution(13710939871913337941)
XLA Ops:
  0.0 0.0 copy-start
  0.0 1.6 copy-done
  1.6 0.0 copy-start.1
  1.6 74.9 %gather_panel.1 = (f32[8,256,256]{2,1,0:T(8,128)S(1)}, f32[5,8,32,256]{3,2,1,0:T(8,128)S(1)}) custom-call(f32[8,256,256]{2,1,0:T(8,128)S(1)} %bitcast.4), custom_call_target="tpu_custom_call" | custom-call | tf_op jit(solution)/shard_map/gather_panel/pallas_call | solution.py:436
  76.5 29.8 %solve_small.1 = (f32[256,256]{1,0:T(8,128)S(1)}, f32[256,256]{1,0:T(8,128)S(1)}, f32[256,256]{1,0:T(8,128)S(1)}, f32[256,256]{1,0:T(8,128)S(1)}, f32[256,256]{1...) custom-call(f32[5,8,32,256]{3,2,1,0:T(8,128)S(1)} %get-tuple-element.18.agb), custom_call_target="tpu_custom_call" | custom-call | tf_op jit(solution)/shard_map/solve_small/pallas_call | solution.py:535
  106.3 43.7 %spread_image.1 = (f32[8,256,256]{2,1,0:T(8,128)S(1)}, f32[1,8,32,256]{3,2,1,0:T(8,128)S(1)}) custom-call(f32[256,256]{1,0:T(8,128)S(1)} %get-tuple-element.19.image, f32[32,256]{1,0:T(8,128)S(1)} %get-tuple-element.20.curv), custom_call_target="tpu_custom_call" | custom-call | tf_op jit(solution)/shard_map/spread_image/pallas_call | solution.py:615
  150.0 0.0 copy-start.2
  150.0 1.3 copy-done.2
  151.3 0.0 copy-done.1
  151.3 8.4 %update_rows.1 = f32[8,256,256]{2,1,0:T(8,128)} custom-call(f32[8,256,256]{2,1,0:T(8,128)S(1)} %bitcast.5, f32[8,256,256]{2,1,0:T(8,128)S(1)} %get-tuple-element.17.prow, f32[8,256,256]{2,1,0:T(8,128)} %copy-done.2, f32[256,256]{1,0:T(8,128)S(1)} %get-tuple-element.22.lt, f32[256,256]{1,0:T(8,128)S(1)} %get-tuple-element.23.y_ref, ...), custom_call_target="tpu_custom_call" | custom-call | tf_op jit(solution)/shard_map/update_rows/pallas_call | solution.py:675
Async XLA Ops:
  0.0 1.6 copy-start
  1.6 149.7 %copy-start.1 = (f32[8,1,256,256]{3,2,1,0:T(8,128)S(1)}, f32[8,1,256,256]{3,2,1,0:T(8,128)}, u32[]{:S(2)}) copy-start(f32[8,1,256,256]{3,2,1,0:T(8,128)} %param.1) | copy-start | bytes 6291460
  150.0 1.3 copy-start.2

commit v2 on v1

--- a/solution.py
+++ b/solution.py
@@ -10,7 +10,9 @@
 NY, NX, NZ, NL, NC = 8, 4, 4, 2, 2
 W = 256
 SUB = 32
-QR = W // 4
+NQ = 8
+QR = W // NQ
+GROUP = 8
 F32, BF16 = jnp.float32, jnp.bfloat16
 MESH = pl.DeviceIdType.MESH
 VMEM_LIMIT = 48 * 1024 * 1024
@@ -144,7 +146,7 @@
             def _():
                 self.arrive(p.y, q)
 
-            @pl.when(jnp.logical_and(jnp.logical_not(p.native), q < 2))
+            @pl.when(jnp.logical_and(jnp.logical_not(p.native), q < NQ // 2))
             def _():
                 self.arrive(p.y, q)
 
@@ -157,62 +159,63 @@
             def _():
                 self.to_l(p.y, q).start()
 
-            @pl.when(jnp.logical_or(p.native, q < 2))
+            @pl.when(jnp.logical_or(p.native, q < NQ // 2))
             def _():
                 self.to_y(0, 0, q).start()
                 self.to_y(1, 0, q).start()
 
-        loop(4, body)
+        loop(NQ, body)
 
     def sends_y(self, side, s, q):
         if s < 3:
-            return jnp.logical_or(self.p.native, q < 2)
+            return jnp.logical_or(self.p.native, q < NQ // 2)
         if side == 0:
-            return q < jnp.where(self.p.native, 2, 1)
-        return jnp.where(self.p.native, q // 2 == 1, q == 1)
+            return q < jnp.where(self.p.native, NQ // 2, NQ // 4)
+        return jnp.where(self.p.native, q, (q % (NQ // 2)) * 2 * (q < NQ // 2)) >= NQ // 2
 
     def ring(self, s):
         p = self.p
-        for side in (0, 1):
-            sign = 1 if side == 0 else -1
-            i = (p.y - sign * s + NY) % NY
-
-            def body(q, side=side, i=i):
-                @pl.when(jnp.logical_or(p.native, q < 2))
-                def _():
+
+        def body(q):
+            for side in (0, 1):
+                sign = 1 if side == 0 else -1
+                i = (p.y - sign * s + NY) % NY
+
+                @pl.when(jnp.logical_or(p.native, q < NQ // 2))
+                def _(i=i):
                     self.arrive(i, q)
 
                 @pl.when(self.sends_y(side, s, q))
-                def _():
+                def _(side=side):
                     self.to_y(side, s, q).start()
 
-                @pl.when(jnp.logical_and(p.native, q >= 2))
-                def _():
+                @pl.when(jnp.logical_and(p.native, q >= NQ // 2))
+                def _(i=i):
                     self.to_l(i, q).start()
 
-            loop(4, body)
+        loop(NQ, body)
 
     def last(self):
         p = self.p
         i = (p.y + 4) % NY
 
         def body(q):
-            @pl.when(jnp.logical_or(p.native, q < 2))
+            @pl.when(jnp.logical_or(p.native, q < NQ // 2))
             def _():
                 self.arrive(i, q)
 
-            @pl.when(jnp.logical_and(p.native, q >= 2))
+            @pl.when(jnp.logical_and(p.native, q >= NQ // 2))
             def _():
                 self.to_l(i, q).start()
 
-        loop(4, body)
+        loop(NQ, body)
 
         @pl.when(jnp.logical_not(p.native))
         def _():
             def late(t):
-                self.arrive(t // 2, 2 + t % 2)
-
-            loop(2 * NY, late)
+                self.arrive(t // (NQ // 2), NQ // 2 + t % (NQ // 2))
+
+            loop(NQ // 2 * NY, late)
 
     def drain(self):
         p = self.p
@@ -234,21 +237,21 @@
             def _():
                 self.to_l(p.y, q).wait_send()
 
-            @pl.when(jnp.logical_and(p.native, q >= 2))
+            @pl.when(jnp.logical_and(p.native, q >= NQ // 2))
             def _():
                 def others(t):
                     self.to_l((p.y + 1 + t) % NY, q).wait_send()
 
                 loop(NY - 1, others)
 
-        loop(4, body)
+        loop(NQ, body)
 
 
 SPREAD_SEMS = [
-    pltpu.SemaphoreType.DMA((NY, 4)),
-    pltpu.SemaphoreType.DMA((3, 4)),
-    pltpu.SemaphoreType.DMA((2, 4, 4)),
-    pltpu.SemaphoreType.DMA((NY, 4)),
+    pltpu.SemaphoreType.DMA((NY, NQ)),
+    pltpu.SemaphoreType.DMA((3, NQ)),
+    pltpu.SemaphoreType.DMA((2, 4, NQ)),
+    pltpu.SemaphoreType.DMA((NY, NQ)),
 ]
 
 
@@ -296,9 +299,11 @@
 
 
 class RowScatter:
-    def __init__(self, place, root, src, dst, recv, send):
-        self.p, self.root, self.src, self.dst = place, root, src, dst
+    def __init__(self, place, root, active, src, dst, recv, send):
+        self.p, self.src, self.dst = place, src, dst
         self.recv, self.send = recv, send
+        self.is_root = jnp.logical_and(place.r == root, active)
+        self.is_leaf = jnp.logical_and(place.r != root, active)
 
     def copy(self, d):
         j = row_piece((self.p.r + d) % (NZ * NC))
@@ -306,19 +311,19 @@
         return rcopy(part, self.dst.at[j], self.send.at[d - 1], self.recv, self.p.at_row(d))
 
     def start(self):
-        @pl.when(self.p.r == self.root)
+        @pl.when(self.is_root)
         def _():
             for d in range(1, 8):
                 self.copy(d).start()
             self.dst[self.p.piece] = self.src[pl.ds(pl.multiple_of(self.p.piece * SUB, SUB), SUB)]
 
     def arrive(self):
-        @pl.when(self.p.r != self.root)
+        @pl.when(self.is_leaf)
         def _():
             self.copy(1).wait_recv()
 
     def finish(self):
-        @pl.when(self.p.r == self.root)
+        @pl.when(self.is_root)
         def _():
             for d in range(1, 8):
                 self.copy(d).wait_send()
@@ -326,17 +331,254 @@
 
 SCATTER_SEMS = [pltpu.SemaphoreType.DMA(()), pltpu.SemaphoreType.DMA((7,))]
 
-GRAM, PROD, FIRST, PANEL, NEXT = range(5)
-
-
-def gather_kernel(a_ref, prow, agb, src, part, rb_core, sums, rb_z, *sems):
-    sp_sems, ge, gl, sc3, sc4, sc2, zs, ar = (
-        sems[0:4], sems[4:6], sems[6:8], sems[8:10], sems[10:12], sems[12:14], sems[14], sems[15:19])
+GRAM, FIRST, PROD, PANEL, NEXT = range(5)
+
+
+class RowReduce:
+    def __init__(self, place, part, rb_core, sums, rb_z, send_c, recv_c, send_z, recv_z):
+        self.p, self.part, self.rb_core, self.sums, self.rb_z = place, part, rb_core, sums, rb_z
+        self.send_z, self.recv_z = send_z, recv_z
+        other = pl.ds(pl.multiple_of((1 - place.h) * NZ, NZ), NZ)
+        self.out = rcopy(part.at[other], rb_core, send_c, recv_c, place.at_core())
+
+    def to_z(self, d):
+        p = self.p
+        return rcopy(self.sums.at[(p.z + d) % NZ], self.rb_z.at[d - 1],
+                     self.send_z.at[d - 1], self.recv_z.at[d - 1], p.at_z(d))
+
+    def start(self):
+        self.out.start()
+
+    def across(self):
+        self.out.wait_recv()
+        mine = pl.ds(pl.multiple_of(self.p.h * NZ, NZ), NZ)
+        self.sums[...] = self.part[mine] + self.rb_core[...]
+        for d in (1, 3, 2):
+            self.to_z(d).start()
+
+    def total(self):
+        total = self.sums[self.p.z]
+        for d in (1, 3, 2):
+            self.to_z(d).wait_recv()
+            total = total + self.rb_z[d - 1]
+        return total
+
+    def finish(self):
+        self.out.wait_send()
+        for d in (1, 2, 3):
+            self.to_z(d).wait_send()
+
+
+REDUCE_BUFS = [
+    pltpu.VMEM((8, SUB, W), F32),
+    pltpu.VMEM((NZ, SUB, W), F32),
+    pltpu.VMEM((NZ, SUB, W), F32),
+    pltpu.VMEM((3, SUB, W), F32),
+]
+REDUCE_SEMS = [pltpu.SemaphoreType.DMA(()), pltpu.SemaphoreType.DMA(()),
+               pltpu.SemaphoreType.DMA((3,)), pltpu.SemaphoreType.DMA((3,))]
+
+
+class EarlyGram:
+    def __init__(self, place, agb, gram, rb, send_r, recv_r, send_x, send_l, send_y, recv):
+        self.p, self.agb, self.gram, self.rb = place, agb, gram, rb
+        self.send_r, self.recv_r = send_r, recv_r
+        self.send_x, self.send_l, self.send_y, self.recv = send_x, send_l, send_y, recv
+        p = place
+        self.root = p.c == 0
+        self.on_x = jnp.logical_and(p.y == 0, p.l == 0)
+        self.on_y = p.y == 0
+
+    def scatter(self, d):
+        j = row_piece((self.p.r + d) % (NZ * NC))
+        return rcopy(self.gram.at[j], self.rb.at[d - 1], self.send_r.at[d - 1], self.recv_r.at[d - 1], self.p.at_row(d))
+
+    def piece(self, send, device):
+        part = self.agb.at[pl.ds(GRAM, 2), self.p.piece]
+        return rcopy(part, part, send, self.recv, device)
+
+    def to_x(self, d):
+        return self.piece(self.send_x.at[d - 1], self.p.at_x(d))
+
+    def to_l(self):
+        return self.piece(self.send_l, self.p.at_l())
+
+    def to_y(self, d):
+        return self.piece(self.send_y.at[d - 1], self.p.at_y(d))
+
+    def local(self, blocks):
+        @pl.when(self.root)
+        def _():
+            self.gram[...] = jnp.zeros_like(self.gram)
+
+            def add(i):
+                block = blocks[i]
+                block = jnp.where(jnp.logical_and(i == 0, self.p.r == 0), 0.0, block)
+                self.gram[...] += dot3(block, block, TN).reshape(8, SUB, W)
+
+            loop(NY, add)
+            for d in range(1, 8):
+                self.scatter(d).start()
+
+    def along_x(self, first):
+        @pl.when(self.root)
+        def _():
+            total = self.gram[self.p.piece]
+            for d in range(1, 8):
+                self.scatter(d).wait_recv()
+                total = total + self.rb[d - 1]
+            self.agb[GRAM, self.p.piece] = total
+        first.arrive()
+
+        @pl.when(self.root)
+        def _():
+            for d in (1, 3, 2):
+                self.to_x(d).start()
+
+    def along_l(self):
+        @pl.when(jnp.logical_and(self.on_x, self.p.x != 0))
+        def _():
+            self.to_l().wait_recv()
+
+        @pl.when(self.on_x)
+        def _():
+            self.to_l().start()
+
+    def along_y(self):
+        @pl.when(jnp.logical_and(self.on_y, self.p.l != 0))
+        def _():
+            self.to_l().wait_recv()
+
+        @pl.when(self.on_y)
+        def _():
+            for d in (4, 3, 5, 2, 6, 1, 7):
+                self.to_y(d).start()
+
+    def arrive(self):
+        @pl.when(jnp.logical_not(self.on_y))
+        def _():
+            self.to_l().wait_recv()
+
+    def finish(self):
+        @pl.when(self.root)
+        def _():
+            for d in range(1, 8):
+                self.scatter(d).wait_send()
+            for d in (1, 2, 3):
+                self.to_x(d).wait_send()
+
+        @pl.when(self.on_x)
+        def _():
+            self.to_l().wait_send()
+
+        @pl.when(self.on_y)
+        def _():
+            for d in range(1, 8):
+                self.to_y(d).wait_send()
+
+
+EARLY_SEMS = [pltpu.SemaphoreType.DMA((7,)), pltpu.SemaphoreType.DMA((7,)), pltpu.SemaphoreType.DMA((3,)),
+              pltpu.SemaphoreType.DMA(()), pltpu.SemaphoreType.DMA((7,)), pltpu.SemaphoreType.DMA(())]
+
+
+def pivot(t, p0, p1, cols, lane, row, jordan):
+    col = cols[0]
+    inv = 1.0 / col[t:t + 1, :]
+    r0 = jnp.where(lane[t:t + 1] == t, 1.0, p0[t:t + 1]) * inv
+    r1 = p1[t:t + 1] * inv
+    here = row == t
+    apply = jnp.logical_not(here) if jordan else row > t
+    factor = jnp.where(apply, col, 0.0)
+    rest = []
+    for other in cols[1:]:
+        ro = other[t:t + 1] * inv
+        new = other - factor * ro
+        rest.append(jnp.where(here, ro, new) if jordan else new)
+    p0 = jnp.where(jnp.logical_and(apply, lane == t), 0.0, p0) - factor * r0
+    p1 = p1 - factor * r1
+    if jordan:
+        p0, p1 = jnp.where(here, r0, p0), jnp.where(here, r1, p1)
+    return p0, p1, rest
+
+
+def group_columns(p0, t):
+    return [jnp.broadcast_to(p0[:, u:u + 1], (SUB, 128)) for u in range(t, t + GROUP)]
+
+
+def turn(v):
+    return jnp.concatenate([v[:, SUB:], v[:, :SUB]], axis=1)
+
+
+def turn_store(ref, body, panel):
+    out = turn(body)
+    ref[:W - SUB, :] = out[SUB:]
+    ref[W - SUB:, :] = turn(panel)
+
+
+def sweep(j, t_ref, m_ref, row_ref, lt_ref):
+    lane = iota((SUB, 128), 1)
+    row = iota((SUB, 128), 0)
+    lane2 = iota((SUB, W), 1)
+    before = row_ref[...]
+    m_left = m_ref[:, :128].T[:SUB] + before
+    q0 = m_ref[:SUB, :128] + jnp.where(lane < SUB, jnp.concatenate(
+        [before[:, :SUB].T, jnp.zeros((SUB, 128 - SUB), F32)], axis=1), 0.0)
+    q1 = m_ref[:SUB, 128:]
+    p0, p1 = t_ref[:SUB, :128], t_ref[:SUB, 128:]
+    for t in range(SUB):
+        if t % GROUP == 0:
+            p_cols, q_cols = group_columns(p0, t), group_columns(q0, t)
+        p0, p1, p_cols = pivot(t, p0, p1, p_cols, lane, row, False)
+        q0, q1, q_cols = pivot(t, q0, q1, q_cols, lane, row, True)
+
+    diag = jnp.sum(jnp.where(lane == row, p0, 0.0), axis=1, keepdims=True)
+    scale = 1.0 / jnp.sqrt(diag)
+    p0, p1 = p0 * scale, p1 * scale
+    upper = jnp.where(lane >= row, p0, 0.0)
+    inside = jnp.where(lane < row, p0, jnp.where(lane == row, scale, 0.0))
+    table = jnp.concatenate([jnp.where(lane < SUB, inside, p0), p1], axis=1)
+    live = jnp.logical_and(lane2 < SUB * (8 - j), lane2 >= 0)
+    upper = jnp.where(live, jnp.concatenate([upper, p1], axis=1), 0.0)
+    first = iota((W, W), 1) < SUB
+    t_new = jnp.where(first, 0.0, t_ref[...]) - packed_tdot(jnp.where(lane2 < SUB, 0.0, upper), table)
+    panel = jnp.concatenate([q0, q1], axis=1)
+    m_new = jnp.where(first, 0.0, m_ref[...]) - packed_tdot(m_left, panel)
+
+    @pl.when(j < 8)
+    def _():
+        turn_store(t_ref, t_new, table)
+        row_ref[...] = upper
+        lt_ref[pl.ds(pl.multiple_of(j * SUB, SUB), SUB), :] = pltpu.roll(upper, j * SUB, 1)
+
+    @pl.when(j > 0)
+    def _():
+        turn_store(m_ref, m_new, panel)
+
+
+class Sems:
+    def __init__(self, refs):
+        self.refs, self.at = refs, 0
+
+    def take(self, group):
+        self.at += len(group)
+        return self.refs[self.at - len(group):self.at]
+
+
+def panel_kernel(a_hbm, prow, lt, y_ref, k_ref, vt_ref, it_ref, image_ref, r_ref, curv_ref,
+                 a_ref, agb, src, near_src, gram, gram_rb, m, row, part, rb_core, sums, rb_z, load, *refs):
+    sems = Sems(refs)
     p = Place()
-    greet([p.at_row(d) for d in range(1, 8)] + [p.at_y(1), p.at_y(NY - 1), p.at_l()]
+
+    def fetch(i):
+        return pltpu.make_async_copy(a_hbm.at[i], a_ref.at[i], load.at[i])
+
+    loop(NY, lambda i: fetch(i).start())
+    greet([p.at_row(d) for d in range(1, 8)] + [p.at_y(d) for d in range(1, 8)] + [p.at_l()]
           + [p.at_x(d) for d in (1, 2, 3)])
-
-    spread = Spread(p, prow, *sp_sems)
+    fetch(0).wait()
+
+    spread_sems = sems.take(SPREAD_SEMS)
+    spread = Spread(p, prow, *spread_sems)
     home_row = p.x * NC + p.l
     home = jnp.logical_and(p.diag, p.r == 0)
 
@@ -348,9 +590,11 @@
     def _():
         src[...] = a_ref[0]
 
+    home_sem = sems.take([0])[0]
+
     def to_home(q):
         rows = pl.ds(pl.multiple_of(q * QR, QR), QR)
-        return rcopy(src.at[rows], prow.at[p.y, rows], zs.at[q], sp_sems[0].at[p.y, q], (home_row, p.c))
+        return rcopy(src.at[rows], prow.at[p.y, rows], home_sem.at[q], spread_sems[0].at[p.y, q], (home_row, p.c))
 
     @pl.when(home)
     def _():
@@ -360,164 +604,78 @@
 
     @pl.when(sends_home)
     def _():
-        loop(4, lambda q: to_home(q).start())
-
-    panel = RowScatter(p, 0, src, agb.at[PANEL], *sc3)
-    following = RowScatter(p, 1, src, agb.at[NEXT], *sc4)
+        loop(NQ, lambda q: to_home(q).start())
+
+    panel = RowScatter(p, 0, p.c >= 0, src, agb.at[PANEL], *sems.take(SCATTER_SEMS))
+    following = RowScatter(p, 1, p.c >= 0, src, agb.at[NEXT], *sems.take(SCATTER_SEMS))
+    first = RowScatter(p, 1, p.c == 0, near_src, agb.at[FIRST], *sems.take(SCATTER_SEMS))
+    early = EarlyGram(p, agb, gram, gram_rb, *sems.take(EARLY_SEMS))
+    columns = RowGather(p, agb, PANEL, NEXT + 1, *sems.take(GATHER_SEMS))
+    grams = RowGather(p, agb, GRAM, FIRST + 1, *sems.take(GATHER_SEMS))
+    prods = RowGather(p, agb, PROD, PROD + 1, *sems.take(GATHER_SEMS))
+    reduce = RowReduce(p, part, rb_core, sums, rb_z, *sems.take(REDUCE_SEMS))
+
     panel.start()
     following.start()
-
+    loop(NY - 1, lambda i: fetch(i + 1).wait())
+
+    @pl.when(jnp.logical_and(p.r == 1, p.c == 0))
+    def _():
+        near_src[...] = a_ref[0].T
+
+    first.start()
+    early.local(a_ref)
     spread.own(home)
+    early.along_x(first)
     panel.arrive()
     following.arrive()
-    early = RowGather(p, agb, PANEL, NEXT + 1, *ge)
-    early.start()
+    columns.start()
     spread.ring(1)
+    early.along_l()
     spread.ring(2)
-    early.relay()
+    early.along_y()
+    columns.relay()
     spread.ring(3)
+    early.arrive()
+    grams.start()
     spread.last()
-
-    first = RowScatter(p, 1, prow.at[0], agb.at[FIRST], *sc2)
-    first.start()
+    columns.finish()
+    grams.relay()
 
     part[...] = jnp.zeros_like(part)
 
     def products(i):
-        block = prow[i]
-        bh, bl = split2(block)
-        ah, al = split2(a_ref[i])
-        gram = mm(bh, bh, NT) + (mm(bh, bl, NT) + mm(bl, bh, NT))
-        prod = mm(bh, ah, NN) + (mm(bh, al, NN) + mm(bl, ah, NN))
-        part[GRAM] += gram.reshape(8, SUB, W)
-        part[PROD] += prod.reshape(8, SUB, W)
+        part[...] += dot3(prow[i], a_ref[i]).reshape(8, SUB, W)
 
     loop(NY, products)
-
-    send_c, recv_c, send_z, recv_z = ar
-    out = rcopy(part.at[:, pl.ds(pl.multiple_of((1 - p.h) * NZ, NZ), NZ)], rb_core, send_c, recv_c, p.at_core())
-    out.start()
-    out.wait_recv()
-    sums[...] = part[:, pl.ds(pl.multiple_of(p.h * NZ, NZ), NZ)] + rb_core[...]
-
-    def to_z(d):
-        return rcopy(sums.at[:, (p.z + d) % NZ], rb_z.at[d - 1], send_z.at[d - 1], recv_z.at[d - 1], p.at_z(d))
-
-    for d in (1, 3, 2):
-        to_z(d).start()
-    total = sums[:, p.z]
-    for d in (1, 3, 2):
-        to_z(d).wait_recv()
-        total = total + rb_z[d - 1]
-    agb[GRAM, p.piece] = total[0]
-    agb[PROD, p.piece] = total[1]
-    first.arrive()
-    late = RowGather(p, agb, GRAM, FIRST + 1, *gl)
-    late.start()
-    early.finish()
-    late.relay()
-    late.finish()
-
-    out.wait_send()
-    for d in (1, 2, 3):
-        to_z(d).wait_send()
-    for each in (panel, following, first):
-        each.finish()
-
-    @pl.when(sends_home)
-    def _():
-        loop(4, lambda q: to_home(q).wait_send())
-
-    spread.drain()
-
-
-def gather_call(slab):
-    whole = pl.BlockSpec(memory_space=pltpu.VMEM)
-    return pl.pallas_call(
-        gather_kernel,
-        out_shape=(jax.ShapeDtypeStruct((NY, W, W), F32), jax.ShapeDtypeStruct((5, 8, SUB, W), F32)),
-        in_specs=[whole],
-        out_specs=(whole, whole),
-        scratch_shapes=[
-            pltpu.VMEM((W, W), F32),
-            pltpu.VMEM((2, 8, SUB, W), F32),
-            pltpu.VMEM((2, NZ, SUB, W), F32),
-            pltpu.VMEM((2, NZ, SUB, W), F32),
-            pltpu.VMEM((3, 2, SUB, W), F32),
-        ]
-        + SPREAD_SEMS + GATHER_SEMS + GATHER_SEMS + SCATTER_SEMS * 3
-        + [pltpu.SemaphoreType.DMA((4,))]
-        + [pltpu.SemaphoreType.DMA(()), pltpu.SemaphoreType.DMA(()),
-           pltpu.SemaphoreType.DMA((3,)), pltpu.SemaphoreType.DMA((3,))],
-        compiler_params=pltpu.CompilerParams(
-            collective_id=0, has_side_effects=True, vmem_limit_bytes=VMEM_LIMIT),
-        name="gather_panel",
-    )(slab)
-
-
-def factor_steps(state, j):
-    j0 = j * SUB
-    rows = iota((SUB, 1), 0)
-    panel = state["s"][j0:j0 + SUB, :]
-    for t in range(SUB):
-        col = panel[:, j0 + t:j0 + t + 1]
-        inv = 1.0 / col[t:t + 1, :]
-        factor = jnp.where(rows > t, col, 0.0)
-        panel = panel - factor * (panel[t:t + 1, :] * inv)
-        yield
-    lanes = iota((SUB, W), 1)
-    diag = jnp.sum(jnp.where(lanes == j0 + iota((SUB, W), 0), panel[:, :W], 0.0), axis=1, keepdims=True)
-    panel = panel * (1.0 / jnp.sqrt(diag))
-    upper = jnp.where(lanes >= j0 + iota((SUB, W), 0), panel[:, :W], 0.0)
-    state["row"] = upper
-    state["lt"][j0:j0 + SUB, :] = upper
-    state["y"][j0:j0 + SUB, :] = panel[:, W:]
-    if j < 7:
-        whole = jnp.concatenate([upper, panel[:, W:]], axis=1)
-        state["s"][j0 + SUB:, :] -= packed_tdot(upper[:, j0 + SUB:] if (j0 + SUB) % 128 == 0 else upper, whole)[
-            (0 if (j0 + SUB) % 128 == 0 else j0 + SUB):, :]
-
-
-def invert_steps(m_ref, row, j):
-    j0 = j * SUB
-    cols = slice(j0, j0 + SUB)
-    m_ref[:, cols] += row.T
-    lanes = iota((SUB, W), 1)
-    rows = iota((SUB, W), 0)
-    panel = m_ref[cols, :]
-    for t in range(SUB):
-        here = lanes == j0 + t
-        col = panel[:, j0 + t:j0 + t + 1]
-        inv = 1.0 / col[t:t + 1, :]
-        pivot = jnp.where(here[t:t + 1, :], 1.0, panel[t:t + 1, :]) * inv
-        panel = jnp.where(rows == t, pivot, jnp.where(here, 0.0, panel) - col * pivot)
-        yield
-    left = m_ref[:, cols].T
-    keep = jnp.logical_and(iota((W, W), 1) >= j0, iota((W, W), 1) < j0 + SUB)
-    m_ref[...] = jnp.where(keep, 0.0, m_ref[...]) - packed_tdot(left, panel)
-    m_ref[cols, :] = panel
-
-
-def solve_kernel(agb, lt, y_ref, k_ref, vt_ref, it_ref, image_ref, r_ref, curv_ref, s, m):
-    p = Place()
-    eye = (iota((W, W), 0) == iota((W, W), 1)).astype(F32)
-    s[:, :W] = agb[GRAM].reshape(W, W)
-    s[:, W:] = eye
+    reduce.start()
+    grams.finish()
+
+    y_ref[...] = agb[GRAM].reshape(W, W)
     m[...] = -agb[FIRST].reshape(W, W)
-    state = dict(s=s, lt=lt, y=y_ref)
-    previous = None
-    for j in range(9):
-        ahead = factor_steps(state, j) if j < 8 else iter(())
-        behind = invert_steps(m, previous, j - 1) if j > 0 else iter(())
-        running = [behind, ahead]
-        while running:
-            for each in list(running):
-                if next(each, running) is running:
-                    running.remove(each)
-        previous = state["row"]
+    row[...] = jnp.zeros_like(row)
+
+    def step(j):
+        sweep(j, y_ref, m, row, lt)
+
+        @pl.when(j == 1)
+        def _():
+            reduce.across()
+
+        @pl.when(j == 4)
+        def _():
+            agb[PROD, p.piece] = reduce.total()
+            prods.start()
+
+        @pl.when(j == 7)
+        def _():
+            prods.relay()
+
+    loop(9, step)
+    prods.finish()
+
     chol_t, inv, near = lt[...], y_ref[...], m[...]
-    panel = agb[PANEL].reshape(W, W)
-    shifted = jnp.where(p.c == 1, chol_t.T, 0.0) - panel
+    shifted = jnp.where(p.c == 1, chol_t.T, 0.0) - agb[PANEL].reshape(W, W)
     vt = dot6(inv, shifted)
     it = agb[NEXT].reshape(W, W) - dot6(inv, agb[PROD].reshape(W, W))
     k_ref[...] = dot6(near, chol_t, NT)
@@ -528,19 +686,42 @@
     mine = vt_ref[pl.ds(pl.multiple_of(p.piece * SUB, SUB), SUB), :]
     curv_ref[...] = dot6(mine, it, NT)
 
-
-def solve_call(agb):
+    reduce.finish()
+    early.finish()
+    for each in (panel, following, first):
+        each.finish()
+
+    @pl.when(sends_home)
+    def _():
+        loop(NQ, lambda q: to_home(q).wait_send())
+
+    spread.drain()
+
+
+def panel_call(slab):
     whole = pl.BlockSpec(memory_space=pltpu.VMEM)
     square = jax.ShapeDtypeStruct((W, W), F32)
+    dma = pltpu.SemaphoreType.DMA
     return pl.pallas_call(
-        solve_kernel,
-        out_shape=(square,) * 7 + (jax.ShapeDtypeStruct((SUB, W), F32),),
-        in_specs=[whole],
-        out_specs=(whole,) * 8,
-        scratch_shapes=[pltpu.VMEM((W, 2 * W), F32), pltpu.VMEM((W, W), F32)],
-        compiler_params=pltpu.CompilerParams(vmem_limit_bytes=VMEM_LIMIT),
-        name="solve_small",
-    )(agb)
+        panel_kernel,
+        out_shape=(jax.ShapeDtypeStruct((NY, W, W), F32),) + (square,) * 7 + (jax.ShapeDtypeStruct((SUB, W), F32),),
+        in_specs=[pl.BlockSpec(memory_space=pl.ANY)],
+        out_specs=(whole,) * 9,
+        scratch_shapes=[
+            pltpu.VMEM((NY, W, W), F32),
+            pltpu.VMEM((5, 8, SUB, W), F32),
+            pltpu.VMEM((W, W), F32),
+            pltpu.VMEM((W, W), F32),
+            pltpu.VMEM((8, SUB, W), F32),
+            pltpu.VMEM((7, SUB, W), F32),
+            pltpu.VMEM((W, W), F32),
+            pltpu.VMEM((SUB, W), F32),
+        ] + REDUCE_BUFS + [dma((NY,))]
+        + SPREAD_SEMS + [dma((NQ,))] + SCATTER_SEMS * 3 + EARLY_SEMS + GATHER_SEMS * 3 + REDUCE_SEMS,
+        compiler_params=pltpu.CompilerParams(
+            collective_id=0, has_side_effects=True, vmem_limit_bytes=VMEM_LIMIT),
+        name="panel_factors",
+    )(slab)
 
 
 def image_kernel(image, curv, irow, cgather, s1, rb1, rb2, s2, rb3, s3, rb4, *sems):
@@ -686,8 +867,7 @@
 
 def on_device(matrix):
     slab = matrix.reshape(NY, W, W)
-    prow, agb = gather_call(slab)
-    lt, y, k, vt, it, image, r, curv = solve_call(agb)
+    prow, lt, y, k, vt, it, image, r, curv = panel_call(slab)
     irow, cgather = image_call(image, curv)
     out = update_call(slab, prow, irow, lt, y, k, vt, it, r, cgather)
     return out.reshape(matrix.shape)

time: 160 us -> 125 us (0.78)
  Pallas kernels: 157 us -> 122 us
    pallas_call x2 -> x1, Pallas kernels: 105 us -> 73.9 us  [panel_call(): pl.pallas_call(panel_kernel, out_shape=(jax.ShapeDtypeStruct((NY, W, W),...]
    pallas_call x1, Pallas kernels: 43.7 us -> 39.3 us  [image_call(): pl.pallas_call(image_kernel, out_shape=(jax.ShapeDtypeStruct((NY, W, W),...]
where the time goes in v2:
time: 125 us
  Pallas kernels  122 us (98%)
  local copies, waits for them, and re-layouts  2.91 us (2%)
    pallas_call x1, Pallas kernels, panel_call(): pl.pallas_call(panel_kernel, out_shape=(jax.ShapeDtypeStruct((NY, W, W),...  73.9 us
    pallas_call x1, Pallas kernels, image_call(): pl.pallas_call(image_kernel, out_shape=(jax.ShapeDtypeStruct((NY, W, W),...  39.3 us
    pallas_call x1, Pallas kernels, update_call(): pl.pallas_call(update_kernel, grid=(NY,), out_shape=jax.ShapeDtypeStruct(...  8.45 us
    unnamed x6, local copies, waits for them, and re-layouts  2.91 us

profile of v2, /device:TPU:1, one launch (start us, length us, event | category | flops | bytes accessed | tf_op | source)
XLA Modules:
  0.0 124.6 jit_solution(3697863553413740956)
XLA Ops:
  0.0 0.0 copy-start
  0.0 1.6 %copy-done = f32[8,1,256,256]{3,2,1,0:T(8,128)S(1)} copy-done((f32[8,1,256,256]{3,2,1,0:T(8,128)S(1)}, f32[8,1,256,256]{3,2,1,0:T(8,128)}, u32[]{:S(2)}) %copy-start) | copy-done | bytes 2097176
  1.6 0.0 copy-start.1
  1.6 73.9 %panel_factors.1 = (f32[8,256,256]{2,1,0:T(8,128)S(1)}, f32[256,256]{1,0:T(8,128)S(1)}, f32[256,256]{1,0:T(8,128)S(1)}, f32[256,256]{1,0:T(8,128)S(1)}, f32[256,...) custom-call(f32[8,256,256]{2,1,0:T(8,128)S(1)} %bitcast.4), custom_call_target="tpu_custom_call" | custom-call | tf_op jit(solution)/shard_map/panel_factors/pallas_call | solution.py:705
  75.5 39.3 %spread_image.1 = (f32[8,256,256]{2,1,0:T(8,128)S(1)}, f32[1,8,32,256]{3,2,1,0:T(8,128)S(1)}) custom-call(f32[256,256]{1,0:T(8,128)S(1)} %get-tuple-element.17.image, f32[32,256]{1,0:T(8,128)S(1)} %get-tuple-element.18.curv), custom_call_target="tpu_custom_call" | custom-call | tf_op jit(solution)/shard_map/spread_image/pallas_call | solution.py:796
  114.8 0.0 copy-start.2
  114.9 1.3 %copy-done.2 = f32[8,256,256]{2,1,0:T(8,128)} copy-done((f32[8,256,256]{2,1,0:T(8,128)}, f32[8,256,256]{2,1,0:T(8,128)S(1)}, u32[]{:S(2)}) %copy-start.2) | copy-done | bytes 2097176
  116.2 0.0 copy-done.1
  116.2 8.4 %update_rows.1 = f32[8,256,256]{2,1,0:T(8,128)} custom-call(f32[8,256,256]{2,1,0:T(8,128)S(1)} %bitcast.5, f32[8,256,256]{2,1,0:T(8,128)S(1)} %get-tuple-element.16.prow, f32[8,256,256]{2,1,0:T(8,128)} %copy-done.2, f32[256,256]{1,0:T(8,128)S(1)} %get-tuple-element.20.lt, f32[256,256]{1,0:T(8,128)S(1)} %get-tuple-element.21.y_ref, ...), custom_call_target="tpu_custom_call" | custom-call | tf_op jit(solution)/shard_map/update_rows/pallas_call | solution.py:856
Async XLA Ops:
  0.0 1.6 %copy-start = (f32[8,1,256,256]{3,2,1,0:T(8,128)S(1)}, f32[8,1,256,256]{3,2,1,0:T(8,128)}, u32[]{:S(2)}) copy-start(f32[8,1,256,256]{3,2,1,0:T(8,128)} %param.1) | copy-start | bytes 6291460
  1.6 114.6 %copy-start.1 = (f32[8,1,256,256]{3,2,1,0:T(8,128)S(1)}, f32[8,1,256,256]{3,2,1,0:T(8,128)}, u32[]{:S(2)}) copy-start(f32[8,1,256,256]{3,2,1,0:T(8,128)} %param.1) | copy-start | bytes 6291460
  114.8 1.3 %copy-start.2 = (f32[8,256,256]{2,1,0:T(8,128)}, f32[8,256,256]{2,1,0:T(8,128)S(1)}, u32[]{:S(2)}) copy-start(f32[8,256,256]{2,1,0:T(8,128)S(1)} %get-tuple-element.19.irow) | copy-start | bytes 6291460

commit v3 on v2

--- a/solution.py
+++ b/solution.py
@@ -125,20 +125,20 @@
         return rcopy(part, part, send, self.recv.at[i, q], device)
 
     def to_x(self, d, q):
-        return self.copy(self.p.y, q, self.send_x.at[d - 1, q], self.p.at_x(d))
+        return self.copy(self.p.y, q, self.send_x.at[d - 1], self.p.at_x(d))
 
     def to_y(self, side, s, q):
         sign = 1 if side == 0 else -1
         i = (self.p.y - sign * s + NY) % NY
-        return self.copy(i, q, self.send_y.at[side, s, q], self.p.at_y(sign + NY))
+        return self.copy(i, q, self.send_y.at[side, s], self.p.at_y(sign + NY))
 
     def to_l(self, i, q):
-        return self.copy(i, q, self.send_l.at[i, q], self.p.at_l())
+        return self.copy(i, q, self.send_l.at[i], self.p.at_l())
 
     def arrive(self, i, q):
-        self.copy(i, q, self.send_l.at[i, q], self.p.at_l()).wait_recv()
-
-    def own(self, home):
+        self.copy(i, q, self.send_l.at[i], self.p.at_l()).wait_recv()
+
+    def own(self, home, beside=lambda q: None):
         p = self.p
 
         def body(q):
@@ -163,6 +163,8 @@
             def _():
                 self.to_y(0, 0, q).start()
                 self.to_y(1, 0, q).start()
+
+            beside(q)
 
         loop(NQ, body)
 
@@ -210,48 +212,45 @@
 
         loop(NQ, body)
 
-        @pl.when(jnp.logical_not(p.native))
-        def _():
-            def late(t):
-                self.arrive(t // (NQ // 2), NQ // 2 + t % (NQ // 2))
-
-            loop(NQ // 2 * NY, late)
+    def late(self, i):
+        @pl.when(jnp.logical_not(self.p.native))
+        def _():
+            loop(NQ // 2, lambda q: self.arrive(i, NQ // 2 + q))
+
+    def sent(self, rows, send):
+        part = self.buf.at[self.p.y, pl.ds(0, rows)]
+        rcopy(part, part, send, self.recv.at[0, 0], self.p.at_l()).wait_send()
 
     def drain(self):
         p = self.p
 
-        def body(q):
-            @pl.when(p.diag)
-            def _():
-                for d in (1, 2, 3):
-                    self.to_x(d, q).wait_send()
-
-            for s in range(4):
-                for side in (0, 1):
-
-                    @pl.when(self.sends_y(side, s, q))
-                    def _(s=s, side=side):
-                        self.to_y(side, s, q).wait_send()
-
-            @pl.when(p.native)
-            def _():
-                self.to_l(p.y, q).wait_send()
-
-            @pl.when(jnp.logical_and(p.native, q >= NQ // 2))
-            def _():
-                def others(t):
-                    self.to_l((p.y + 1 + t) % NY, q).wait_send()
-
-                loop(NY - 1, others)
-
-        loop(NQ, body)
+        @pl.when(p.diag)
+        def _():
+            for d in range(3):
+                self.sent(W, self.send_x.at[d])
+
+        def ring(full):
+            for side in (0, 1):
+                for s in range(3):
+                    self.sent(full, self.send_y.at[side, s])
+                self.sent(full // 2, self.send_y.at[side, 3])
+
+        @pl.when(p.native)
+        def _():
+            ring(W)
+            self.sent(W, self.send_l.at[p.y])
+            loop(NY - 1, lambda t: self.sent(W // 2, self.send_l.at[(p.y + 1 + t) % NY]))
+
+        @pl.when(jnp.logical_not(p.native))
+        def _():
+            ring(W // 2)
 
 
 SPREAD_SEMS = [
     pltpu.SemaphoreType.DMA((NY, NQ)),
-    pltpu.SemaphoreType.DMA((3, NQ)),
-    pltpu.SemaphoreType.DMA((2, 4, NQ)),
-    pltpu.SemaphoreType.DMA((NY, NQ)),
+    pltpu.SemaphoreType.DMA((3,)),
+    pltpu.SemaphoreType.DMA((2, 4)),
+    pltpu.SemaphoreType.DMA((NY,)),
 ]
 
 
@@ -406,17 +405,16 @@
     def to_y(self, d):
         return self.piece(self.send_y.at[d - 1], self.p.at_y(d))
 
-    def local(self, blocks):
+    def add(self, block, i):
         @pl.when(self.root)
         def _():
-            self.gram[...] = jnp.zeros_like(self.gram)
-
-            def add(i):
-                block = blocks[i]
-                block = jnp.where(jnp.logical_and(i == 0, self.p.r == 0), 0.0, block)
-                self.gram[...] += dot3(block, block, TN).reshape(8, SUB, W)
-
-            loop(NY, add)
+            mine = jnp.where(jnp.logical_and(i == 0, self.p.r == 0), 0.0, block)
+            prod = dot3(mine.T, mine).reshape(8, SUB, W)
+            self.gram[...] = jnp.where(i == 0, prod, self.gram[...] + prod)
+
+    def start(self):
+        @pl.when(self.root)
+        def _():
             for d in range(1, 8):
                 self.scatter(d).start()
 
@@ -555,6 +553,80 @@
         turn_store(m_ref, m_new, panel)
 
 
+class ColumnSums:
+    def __init__(self, place, out, mine, s1, s2, s3, rows, rb1, rb2, rb3, c1, c2, c3, c4, gather):
+        self.p, self.out, self.mine, self.rows = place, out, mine, rows
+        self.s1, self.s2, self.s3 = s1, s2, s3
+        self.rb1, self.rb2, self.rb3 = rb1, rb2, rb3
+        self.c1, self.c2, self.c3, self.c4 = c1, c2, c3, c4
+        self.gather = RowGather(place, out, 0, 3, *gather)
+        self.here = pl.ds(pl.multiple_of(place.x * 8, 8), 8)
+
+    def to_l(self):
+        return rcopy(self.mine, self.rb1, self.c1.at[0], self.c1.at[1], self.p.at_l())
+
+    def to_x(self, d):
+        x = (self.p.x + d) % NX
+        part = self.s1.at[:, pl.ds(pl.multiple_of(x * 8, 8), 8)]
+        return rcopy(part, self.rb2.at[d - 1], self.c2.at[0, d - 1], self.c2.at[1, d - 1], self.p.at_x(d))
+
+    def to_y(self, d):
+        return rcopy(self.s2, self.rb3.at[d - 1], self.c3.at[0, d - 1], self.c3.at[1, d - 1], self.p.at_y(d))
+
+    def back_x(self, d):
+        part = self.rows.at[:, self.here]
+        return rcopy(self.s3, part, self.c4.at[0, d - 1], self.c4.at[1, d - 1], self.p.at_x(d))
+
+    def along_l(self):
+        self.to_l().start()
+
+    def along_x(self):
+        self.to_l().wait_recv()
+        self.s1[...] = self.mine[...] + self.rb1[...]
+        for d in (1, 3, 2):
+            self.to_x(d).start()
+
+    def along_y(self):
+        total = self.s1[:, self.here]
+        for d in (1, 2, 3):
+            self.to_x(d).wait_recv()
+            total = total + self.rb2[d - 1]
+        self.s2[...] = total
+        for d in (4, 3, 5, 2, 6, 1, 7):
+            self.to_y(d).start()
+
+    def return_x(self):
+        total = self.s2[...]
+        for d in range(1, 8):
+            self.to_y(d).wait_recv()
+            total = total + self.rb3[d - 1]
+        self.s3[...] = total
+        self.rows[:, self.here] = total
+        for d in (1, 3, 2):
+            self.back_x(d).start()
+
+    def along_row(self):
+        for d in (1, 2, 3):
+            self.back_x(d).wait_recv()
+        self.out[:, self.p.piece] = self.rows[...]
+        self.gather.start()
+
+    def finish(self):
+        self.to_l().wait_send()
+        for d in (1, 2, 3):
+            self.to_x(d).wait_send()
+            self.back_x(d).wait_send()
+        for d in range(1, 8):
+            self.to_y(d).wait_send()
+
+
+SUM_BUFS = [pltpu.VMEM((3, 8, SUB, W), F32), pltpu.VMEM((3, SUB, W), F32), pltpu.VMEM((3, SUB, W), F32),
+            pltpu.VMEM((3, 8, W), F32), pltpu.VMEM((3, 8, W), F32), pltpu.VMEM((3, SUB, W), F32),
+            pltpu.VMEM((3, SUB, W), F32), pltpu.VMEM((3, 3, 8, W), F32), pltpu.VMEM((7, 3, 8, W), F32)]
+SUM_SEMS = [pltpu.SemaphoreType.DMA((2,)), pltpu.SemaphoreType.DMA((2, 3)),
+            pltpu.SemaphoreType.DMA((2, 7)), pltpu.SemaphoreType.DMA((2, 3))]
+
+
 class Sems:
     def __init__(self, refs):
         self.refs, self.at = refs, 0
@@ -564,9 +636,9 @@
         return self.refs[self.at - len(group):self.at]
 
 
-def panel_kernel(a_hbm, prow, lt, y_ref, k_ref, vt_ref, it_ref, image_ref, r_ref, curv_ref,
-                 a_ref, agb, src, near_src, gram, gram_rb, m, row, part, rb_core, sums, rb_z, load, *refs):
+def panel_kernel(a_hbm, out, a_ref, prow, irow, lt, y_ref, k_ref, it_ref, r_ref, s_ref, u_ref, agb, src, near_src, gram, gram_rb, m, row, part, rb_core, sums, rb_z, load, store, *refs):
     sems = Sems(refs)
+    sum_bufs = sems.take(SUM_BUFS)
     p = Place()
 
     def fetch(i):
@@ -611,7 +683,8 @@
     first = RowScatter(p, 1, p.c == 0, near_src, agb.at[FIRST], *sems.take(SCATTER_SEMS))
     early = EarlyGram(p, agb, gram, gram_rb, *sems.take(EARLY_SEMS))
     columns = RowGather(p, agb, PANEL, NEXT + 1, *sems.take(GATHER_SEMS))
-    grams = RowGather(p, agb, GRAM, FIRST + 1, *sems.take(GATHER_SEMS))
+    grams = RowGather(p, agb, GRAM, GRAM + 1, *sems.take(GATHER_SEMS))
+    firsts = RowGather(p, agb, FIRST, FIRST + 1, *sems.take(GATHER_SEMS))
     prods = RowGather(p, agb, PROD, PROD + 1, *sems.take(GATHER_SEMS))
     reduce = RowReduce(p, part, rb_core, sums, rb_z, *sems.take(REDUCE_SEMS))
 
@@ -624,68 +697,135 @@
         near_src[...] = a_ref[0].T
 
     first.start()
-    early.local(a_ref)
-    spread.own(home)
-    early.along_x(first)
+
+    def product(i, half):
+        rows = pl.ds(half * (W // 2), W // 2)
+        part[half * NZ:(half + 1) * NZ] += dot3(prow[i, rows], a_ref[i]).reshape(NZ, SUB, W)
+
+    def products(*offsets):
+        for d in offsets:
+            product((p.y + d) % NY, 0)
+
+        @pl.when(p.native)
+        def _():
+            for d in offsets:
+                product((p.y + d) % NY, 1)
+
+    part[...] = jnp.zeros_like(part)
+    spread.own(home, lambda q: early.add(a_ref[q], q))
+    early.start()
     panel.arrive()
     following.arrive()
     columns.start()
     spread.ring(1)
+    early.along_x(first)
+    products(0)
+    spread.ring(2)
     early.along_l()
-    spread.ring(2)
+    columns.relay()
+    products(1, 7)
+    spread.ring(3)
     early.along_y()
-    columns.relay()
-    spread.ring(3)
+    spread.last()
+    products(2, 6)
     early.arrive()
     grams.start()
-    spread.last()
+    firsts.start()
+    products(3, 5, 4)
+
+    @pl.when(jnp.logical_not(p.native))
+    def _():
+        def rest(t):
+            i = (p.y + t) % NY
+            spread.late(i)
+            product(i, 1)
+
+        loop(NY, rest)
+
+    reduce.start()
     columns.finish()
     grams.relay()
-
-    part[...] = jnp.zeros_like(part)
-
-    def products(i):
-        part[...] += dot3(prow[i], a_ref[i]).reshape(8, SUB, W)
-
-    loop(NY, products)
-    reduce.start()
+    reduce.across()
     grams.finish()
+    firsts.relay()
 
     y_ref[...] = agb[GRAM].reshape(W, W)
-    m[...] = -agb[FIRST].reshape(W, W)
     row[...] = jnp.zeros_like(row)
+    colsum = ColumnSums(p, *sum_bufs, *sems.take(SUM_SEMS), sems.take(GATHER_SEMS))
+    images = Spread(p, irow, *sems.take(SPREAD_SEMS))
 
     def step(j):
         sweep(j, y_ref, m, row, lt)
 
+        @pl.when(j == 0)
+        def _():
+            firsts.finish()
+            m[...] = -agb[FIRST].reshape(W, W)
+
         @pl.when(j == 1)
         def _():
-            reduce.across()
+            total = reduce.total()
+            agb[PROD, p.piece] = total
+            prods.start()
+            colsum.mine[0] = dot6(total, agb[PANEL].reshape(W, W), NT)
+            colsum.mine[1] = jnp.where(p.c == 1, total, 0.0)
+            colsum.mine[2] = jnp.where(p.c == 1, agb[NEXT, p.piece], 0.0)
+            colsum.along_l()
+
+        @pl.when(j == 3)
+        def _():
+            colsum.along_x()
 
         @pl.when(j == 4)
         def _():
-            agb[PROD, p.piece] = reduce.total()
-            prods.start()
-
-        @pl.when(j == 7)
-        def _():
             prods.relay()
+
+        @pl.when(j == 5)
+        def _():
+            colsum.along_y()
+
+        @pl.when(j == 8)
+        def _():
+            colsum.return_x()
 
     loop(9, step)
     prods.finish()
 
-    chol_t, inv, near = lt[...], y_ref[...], m[...]
-    shifted = jnp.where(p.c == 1, chol_t.T, 0.0) - agb[PANEL].reshape(W, W)
-    vt = dot6(inv, shifted)
-    it = agb[NEXT].reshape(W, W) - dot6(inv, agb[PROD].reshape(W, W))
-    k_ref[...] = dot6(near, chol_t, NT)
-    r_ref[...] = dot6(near, shifted)
-    vt_ref[...] = vt
-    it_ref[...] = it
-    image_ref[...] = it.T
-    mine = vt_ref[pl.ds(pl.multiple_of(p.piece * SUB, SUB), SUB), :]
-    curv_ref[...] = dot6(mine, it, NT)
-
+    it_ref[...] = agb[NEXT].reshape(W, W) - dot6(y_ref[...], agb[PROD].reshape(W, W))
+
+    @pl.when(p.diag)
+    def _():
+        irow[p.y] = it_ref[...].T
+        images.own(p.diag)
+
+    colsum.along_row()
+    shifted = jnp.where(p.c == 1, lt[...].T, 0.0) - agb[PANEL].reshape(W, W)
+    r_ref[...] = dot6(m[...], shifted)
+
+    @pl.when(jnp.logical_not(p.diag))
+    def _():
+        images.own(p.diag)
+
+    k_ref[...] = dot6(m[...], lt[...], NT)
+
+    def away(i, half):
+        rows = pl.ds(half * (W // 2), W // 2)
+        a_ref[i, rows] -= dot3(irow[i, rows], r_ref[...])
+
+    def aways(*offsets):
+        for d in offsets:
+            away((p.y + d) % NY, 0)
+
+        @pl.when(p.native)
+        def _():
+            for d in offsets:
+                away((p.y + d) % NY, 1)
+
+    def flip(i):
+        prow[i] = prow[i].T
+
+    spread.drain()
+    images.ring(1)
     reduce.finish()
     early.finish()
     for each in (panel, following, first):
@@ -695,182 +835,85 @@
     def _():
         loop(NQ, lambda q: to_home(q).wait_send())
 
-    spread.drain()
+    loop(4, flip)
+    aways(0)
+    images.ring(2)
+    colsum.gather.relay()
+    loop(4, lambda i: flip(4 + i))
+    aways(1, 7)
+    images.ring(3)
+    images.last()
+    aways(2, 6, 3, 5, 4)
+    colsum.gather.finish()
+    inv = y_ref[...]
+    far = dot3(inv, r_ref[...], TN)
+    prod = colsum.out[1].reshape(W, W)
+    bent = dot3(inv, dot3(colsum.out[0].reshape(W, W), far) - dot3(prod, r_ref[...]))
+    bent = bent + (dot3(colsum.out[2].reshape(W, W), r_ref[...]) - dot3(prod, far, TN))
+    s_ref[...] = dot3(k_ref[...], it_ref[...] - bent, TN)
+    u_ref[...] = dot3(inv, s_ref[...], TN)
+
+    def put(i):
+        return pltpu.make_async_copy(a_ref.at[i], out.at[i], store.at[i])
+
+    def update(t):
+        i = (p.y + t) % NY
+        images.late(i)
+
+        @pl.when(jnp.logical_not(p.native))
+        def _():
+            away(i, 1)
+
+        b = i * (NZ * NC) + p.r
+        old = a_ref[i]
+        new = old + dot3(prow[i], u_ref[...])
+        a_ref[i] = jnp.where(b == 1, new - s_ref[...], new)
+
+        @pl.when(p.c == 0)
+        def _():
+            a_ref[i] = jnp.where(b == 0, old, jnp.where(b == 1, lt[...], 0.0))
+
+        @pl.when(jnp.logical_and(p.c > 0, b == 0))
+        def _():
+            a_ref[i] = jnp.where(p.c == 1, lt[...].T, 0.0)
+
+        put(i).start()
+
+    loop(NY, update)
+    colsum.finish()
+    images.drain()
+    loop(NY, lambda i: put(i).wait())
 
 
 def panel_call(slab):
-    whole = pl.BlockSpec(memory_space=pltpu.VMEM)
-    square = jax.ShapeDtypeStruct((W, W), F32)
     dma = pltpu.SemaphoreType.DMA
+    square = pltpu.VMEM((W, W), F32)
+    blocks = pltpu.VMEM((NY, W, W), F32)
     return pl.pallas_call(
         panel_kernel,
-        out_shape=(jax.ShapeDtypeStruct((NY, W, W), F32),) + (square,) * 7 + (jax.ShapeDtypeStruct((SUB, W), F32),),
-        in_specs=[pl.BlockSpec(memory_space=pl.ANY)],
-        out_specs=(whole,) * 9,
-        scratch_shapes=[
-            pltpu.VMEM((NY, W, W), F32),
+        out_shape=jax.ShapeDtypeStruct((NY, W, W), F32),
+        in_specs=[pl.BlockSpec(memory_space=pltpu.HBM)],
+        out_specs=pl.BlockSpec(memory_space=pl.ANY),
+        scratch_shapes=[blocks] * 3 + [square] * 7 + [
             pltpu.VMEM((5, 8, SUB, W), F32),
-            pltpu.VMEM((W, W), F32),
-            pltpu.VMEM((W, W), F32),
+            square,
+            square,
             pltpu.VMEM((8, SUB, W), F32),
             pltpu.VMEM((7, SUB, W), F32),
-            pltpu.VMEM((W, W), F32),
+            square,
             pltpu.VMEM((SUB, W), F32),
-        ] + REDUCE_BUFS + [dma((NY,))]
-        + SPREAD_SEMS + [dma((NQ,))] + SCATTER_SEMS * 3 + EARLY_SEMS + GATHER_SEMS * 3 + REDUCE_SEMS,
+        ] + REDUCE_BUFS + [dma((NY,)), dma((NY,))] + SUM_BUFS
+        + SPREAD_SEMS + [dma((NQ,))] + SCATTER_SEMS * 3 + EARLY_SEMS + GATHER_SEMS * 4 + REDUCE_SEMS
+        + SUM_SEMS + GATHER_SEMS + SPREAD_SEMS,
         compiler_params=pltpu.CompilerParams(
             collective_id=0, has_side_effects=True, vmem_limit_bytes=VMEM_LIMIT),
-        name="panel_factors",
+        name="panel_step",
     )(slab)
-
-
-def image_kernel(image, curv, irow, cgather, s1, rb1, rb2, s2, rb3, s3, rb4, *sems):
-    sp_sems, ge, c1, c2, c3, c4 = sems[0:4], sems[4:6], sems[6:8], sems[8:10], sems[10:12], sems[12:14]
-    p = Place()
-    greet([p.at_row(d) for d in range(1, 8)] + [p.at_y(d) for d in range(1, 8)] + [p.at_l()]
-          + [p.at_x(d) for d in (1, 2, 3)])
-    spread = Spread(p, irow, *sp_sems)
-
-    @pl.when(p.diag)
-    def _():
-        irow[p.y] = image[...]
-
-    def to_l():
-        return rcopy(curv, rb1, c1[0], c1[1], p.at_l())
-
-    def to_x(d):
-        x = (p.x + d) % NX
-        return rcopy(s1.at[pl.ds(pl.multiple_of(x * 8, 8), 8)], rb2.at[d - 1], c2[0].at[d - 1], c2[1].at[d - 1], p.at_x(d))
-
-    def to_y(d):
-        return rcopy(s2, rb3.at[d - 1], c3[0].at[d - 1], c3[1].at[d - 1], p.at_y(d))
-
-    def back_x(d):
-        rows = pl.ds(pl.multiple_of(p.x * 8, 8), 8)
-        return rcopy(s3, rb4.at[rows], c4[0].at[d - 1], c4[1].at[d - 1], p.at_x(d))
-
-    to_l().start()
-    spread.own(p.diag)
-    to_l().wait_recv()
-    s1[...] = curv[...] + rb1[...]
-    for d in (1, 2, 3):
-        to_x(d).start()
-    spread.ring(1)
-    total = s1[pl.ds(pl.multiple_of(p.x * 8, 8), 8)]
-    for d in (1, 2, 3):
-        to_x(d).wait_recv()
-        total = total + rb2[d - 1]
-    s2[...] = total
-    for d in range(1, 8):
-        to_y(d).start()
-    spread.ring(2)
-    total = s2[...]
-    for d in range(1, 8):
-        to_y(d).wait_recv()
-        total = total + rb3[d - 1]
-    s3[...] = total
-    for d in (1, 2, 3):
-        back_x(d).start()
-    rb4[pl.ds(pl.multiple_of(p.x * 8, 8), 8)] = total
-    spread.ring(3)
-    for d in (1, 2, 3):
-        back_x(d).wait_recv()
-    cgather[0, p.piece] = rb4[...]
-    gather = RowGather(p, cgather, 0, 1, *ge)
-    gather.start()
-    spread.last()
-    gather.relay()
-    gather.finish()
-    to_l().wait_send()
-    for d in (1, 2, 3):
-        to_x(d).wait_send()
-        back_x(d).wait_send()
-    for d in range(1, 8):
-        to_y(d).wait_send()
-    spread.drain()
-
-
-def image_call(image, curv):
-    whole = pl.BlockSpec(memory_space=pltpu.VMEM)
-    dma = pltpu.SemaphoreType.DMA
-    return pl.pallas_call(
-        image_kernel,
-        out_shape=(jax.ShapeDtypeStruct((NY, W, W), F32), jax.ShapeDtypeStruct((1, 8, SUB, W), F32)),
-        in_specs=[whole, whole],
-        out_specs=(whole, whole),
-        scratch_shapes=[
-            pltpu.VMEM((SUB, W), F32),
-            pltpu.VMEM((SUB, W), F32),
-            pltpu.VMEM((3, 8, W), F32),
-            pltpu.VMEM((8, W), F32),
-            pltpu.VMEM((7, 8, W), F32),
-            pltpu.VMEM((8, W), F32),
-            pltpu.VMEM((SUB, W), F32),
-        ]
-        + SPREAD_SEMS + GATHER_SEMS
-        + [dma(()), dma(()), dma((3,)), dma((3,)), dma((7,)), dma((7,)), dma((3,)), dma((3,))],
-        compiler_params=pltpu.CompilerParams(
-            collective_id=1, has_side_effects=True, vmem_limit_bytes=VMEM_LIMIT),
-        name="spread_image",
-    )(image, curv)
-
-
-def update_kernel(a_ref, prow, irow, lt, y_ref, k_ref, vt_ref, it_ref, r_ref, curv, out, s_ref, u_ref, rn_ref):
-    p = Place()
-    i = pl.program_id(0)
-
-    @pl.when(i == 0)
-    def _():
-        kern = k_ref[...]
-        inner = dot3(dot3(kern, curv[0].reshape(W, W), TN), kern)
-        s = dot3(kern, it_ref[...], TN) - 0.5 * dot3(inner + inner.T, vt_ref[...])
-        s_ref[...] = s
-        uh, ul = split2(dot3(y_ref[...], s, TN))
-        u_ref[0] = uh
-        u_ref[1] = ul
-        rh, rl = split2(r_ref[...])
-        rn_ref[0] = rh
-        rn_ref[1] = rl
-
-    ph, plo = split2(prow[0])
-    ih, il = split2(irow[0])
-    first = mm(ph, u_ref[0], TN) + (mm(ph, u_ref[1], TN) + mm(plo, u_ref[0], TN))
-    second = mm(ih, rn_ref[0], NN) + (mm(ih, rn_ref[1], NN) + mm(il, rn_ref[0], NN))
-    b = i * (NZ * NC) + p.r
-    res = a_ref[0] + (first - second)
-    res = jnp.where(b == 1, res - s_ref[...], res)
-    out[0] = res
-
-    @pl.when(p.c == 0)
-    def _():
-        out[0] = jnp.where(b == 0, a_ref[0], jnp.where(b == 1, lt[...], 0.0))
-
-    @pl.when(jnp.logical_and(p.c > 0, b == 0))
-    def _():
-        out[0] = jnp.where(p.c == 1, lt[...].T, 0.0)
-
-
-def update_call(slab, prow, irow, lt, y, k, vt, it, r, curv):
-    tile = pl.BlockSpec((1, W, W), lambda i: (i, 0, 0))
-    square = pl.BlockSpec((W, W), lambda i: (0, 0))
-    return pl.pallas_call(
-        update_kernel,
-        grid=(NY,),
-        out_shape=jax.ShapeDtypeStruct((NY, W, W), F32),
-        in_specs=[tile, tile, tile] + [square] * 6 + [pl.BlockSpec((1, 8, SUB, W), lambda i: (0, 0, 0, 0))],
-        out_specs=tile,
-        scratch_shapes=[pltpu.VMEM((W, W), F32), pltpu.VMEM((2, W, W), BF16), pltpu.VMEM((2, W, W), BF16)],
-        compiler_params=pltpu.CompilerParams(vmem_limit_bytes=VMEM_LIMIT),
-        name="update_rows",
-    )(slab, prow, irow, lt, y, k, vt, it, r, curv)
 
 
 def on_device(matrix):
     slab = matrix.reshape(NY, W, W)
-    prow, lt, y, k, vt, it, image, r, curv = panel_call(slab)
-    irow, cgather = image_call(image, curv)
-    out = update_call(slab, prow, irow, lt, y, k, vt, it, r, cgather)
-    return out.reshape(matrix.shape)
+    return panel_call(slab).reshape(matrix.shape)
 
 
 def solution(mesh):

time: 125 us -> 115 us (0.920)
  the two profiles are of different devices: /device:TPU:1 before, /device:TPU:68 now
where the time goes in v3:
time: 115 us
  Pallas kernels  112 us (97%)
  local copies, waits for them, and re-layouts  2.91 us (3%)
    pallas_call x1, Pallas kernels, panel_call(): pl.pallas_call(panel_kernel, out_shape=jax.ShapeDtypeStruct((NY, W, W), F...  112 us
    unnamed x3, local copies, waits for them, and re-layouts  2.91 us

profile of v3, /device:TPU:68, one launch (start us, length us, event | category | flops | bytes accessed | tf_op | source)
XLA Modules:
  0.0 114.8 jit_solution(14142520589341239110)
XLA Ops:
  0.0 0.0 copy-start
  0.0 1.6 %copy-done = f32[8,1,256,256]{3,2,1,0:T(8,128)S(1)} copy-done((f32[8,1,256,256]{3,2,1,0:T(8,128)S(1)}, f32[8,1,256,256]{3,2,1,0:T(8,128)}, u32[]{:S(2)}) %copy-start) | copy-done | bytes 2097176
  1.6 111.9 %panel_step.1 = f32[8,256,256]{2,1,0:T(8,128)S(1)} custom-call(f32[8,256,256]{2,1,0:T(8,128)S(1)} %bitcast.5), custom_call_target="tpu_custom_call" | custom-call | tf_op jit(solution)/shard_map/panel_step/pallas_call | solution.py:892
  113.5 1.3 %copy.4 = f32[8,1,256,256]{3,2,1,0:T(8,128)} copy(f32[8,1,256,256]{3,2,1,0:T(8,128)S(1)} %bitcast.4) | data formatting | bytes 4194304
Async XLA Ops:
  0.0 1.6 %copy-start = (f32[8,1,256,256]{3,2,1,0:T(8,128)S(1)}, f32[8,1,256,256]{3,2,1,0:T(8,128)}, u32[]{:S(2)}) copy-start(f32[8,1,256,256]{3,2,1,0:T(8,128)} %param.1) | copy-start | bytes 6291460

commit v4 on v3

--- a/solution.py
+++ b/solution.py
@@ -15,7 +15,7 @@
 GROUP = 8
 F32, BF16 = jnp.float32, jnp.bfloat16
 MESH = pl.DeviceIdType.MESH
-VMEM_LIMIT = 48 * 1024 * 1024
+VMEM_LIMIT = 50 * 1024 * 1024
 NN = (((1,), (0,)), ((), ()))
 NT = (((1,), (1,)), ((), ()))
 TN = (((0,), (0,)), ((), ()))
@@ -636,7 +636,7 @@
         return self.refs[self.at - len(group):self.at]
 
 
-def panel_kernel(a_hbm, out, a_ref, prow, irow, lt, y_ref, k_ref, it_ref, r_ref, s_ref, u_ref, agb, src, near_src, gram, gram_rb, m, row, part, rb_core, sums, rb_z, load, store, *refs):
+def panel_kernel(a_hbm, out, a_ref, prow, irow, lt, y_ref, k_ref, it_ref, r_ref, s_ref, u_ref, agb, src, near_src, gram, gram_rb, m, row, part, rb_core, sums, rb_z, load, *refs):
     sems = Sems(refs)
     sum_bufs = sems.take(SUM_BUFS)
     p = Place()
@@ -726,8 +726,8 @@
     products(1, 7)
     spread.ring(3)
     early.along_y()
+    products(2, 6)
     spread.last()
-    products(2, 6)
     early.arrive()
     grams.start()
     firsts.start()
@@ -842,8 +842,10 @@
     loop(4, lambda i: flip(4 + i))
     aways(1, 7)
     images.ring(3)
+    colsum.finish()
+    aways(2, 6)
     images.last()
-    aways(2, 6, 3, 5, 4)
+    aways(3, 5, 4)
     colsum.gather.finish()
     inv = y_ref[...]
     far = dot3(inv, r_ref[...], TN)
@@ -853,9 +855,6 @@
     s_ref[...] = dot3(k_ref[...], it_ref[...] - bent, TN)
     u_ref[...] = dot3(inv, s_ref[...], TN)
 
-    def put(i):
-        return pltpu.make_async_copy(a_ref.at[i], out.at[i], store.at[i])
-
     def update(t):
         i = (p.y + t) % NY
         images.late(i)
@@ -867,22 +866,18 @@
         b = i * (NZ * NC) + p.r
         old = a_ref[i]
         new = old + dot3(prow[i], u_ref[...])
-        a_ref[i] = jnp.where(b == 1, new - s_ref[...], new)
+        out[i] = jnp.where(b == 1, new - s_ref[...], new)
 
         @pl.when(p.c == 0)
         def _():
-            a_ref[i] = jnp.where(b == 0, old, jnp.where(b == 1, lt[...], 0.0))
+            out[i] = jnp.where(b == 0, old, jnp.where(b == 1, lt[...], 0.0))
 
         @pl.when(jnp.logical_and(p.c > 0, b == 0))
         def _():
-            a_ref[i] = jnp.where(p.c == 1, lt[...].T, 0.0)
-
-        put(i).start()
+            out[i] = jnp.where(p.c == 1, lt[...].T, 0.0)
 
     loop(NY, update)
-    colsum.finish()
     images.drain()
-    loop(NY, lambda i: put(i).wait())
 
 
 def panel_call(slab):
@@ -892,8 +887,8 @@
     return pl.pallas_call(
         panel_kernel,
         out_shape=jax.ShapeDtypeStruct((NY, W, W), F32),
-        in_specs=[pl.BlockSpec(memory_space=pltpu.HBM)],
-        out_specs=pl.BlockSpec(memory_space=pl.ANY),
+        in_specs=[pl.BlockSpec(memory_space=pl.ANY)],
+        out_specs=pl.BlockSpec(memory_space=pltpu.VMEM),
         scratch_shapes=[blocks] * 3 + [square] * 7 + [
             pltpu.VMEM((5, 8, SUB, W), F32),
             square,
@@ -902,7 +897,7 @@
             pltpu.VMEM((7, SUB, W), F32),
             square,
             pltpu.VMEM((SUB, W), F32),
-        ] + REDUCE_BUFS + [dma((NY,)), dma((NY,))] + SUM_BUFS
+        ] + REDUCE_BUFS + [dma((NY,))] + SUM_BUFS
         + SPREAD_SEMS + [dma((NQ,))] + SCATTER_SEMS * 3 + EARLY_SEMS + GATHER_SEMS * 4 + REDUCE_SEMS
         + SUM_SEMS + GATHER_SEMS + SPREAD_SEMS,
         compiler_params=pltpu.CompilerParams(

time: 115 us -> 114 us (level)
  the two profiles are of different devices: /device:TPU:68 before, /device:TPU:66 now
where the time goes in v4:
time: 114 us
  Pallas kernels  112 us (98%)
  local copies, waits for them, and re-layouts  1.32 us (1%)
    pallas_call x1, Pallas kernels, panel_call(): pl.pallas_call(panel_kernel, out_shape=jax.ShapeDtypeStruct((NY, W, W), F...  112 us

profile of v4, /device:TPU:66, one launch (start us, length us, event | category | flops | bytes accessed | tf_op | source)
XLA Modules:
  0.0 113.7 jit_solution(10634171865254839834)
XLA Ops:
  0.0 112.4 %panel_step.1 = f32[8,256,256]{2,1,0:T(8,128)S(1)} custom-call(f32[8,256,256]{2,1,0:T(8,128)} %bitcast.5), custom_call_target="tpu_custom_call" | custom-call | tf_op jit(solution)/shard_map/panel_step/pallas_call | solution.py:887
  112.4 1.3 %copy.4 = f32[8,1,256,256]{3,2,1,0:T(8,128)} copy(f32[8,1,256,256]{3,2,1,0:T(8,128)S(1)} %bitcast.4) | data formatting | bytes 4194304

commit v5 on v4

--- a/solution.py
+++ b/solution.py
@@ -799,12 +799,12 @@
         images.own(p.diag)
 
     colsum.along_row()
+    @pl.when(jnp.logical_not(p.diag))
+    def _():
+        images.own(p.diag)
+
     shifted = jnp.where(p.c == 1, lt[...].T, 0.0) - agb[PANEL].reshape(W, W)
     r_ref[...] = dot6(m[...], shifted)
-
-    @pl.when(jnp.logical_not(p.diag))
-    def _():
-        images.own(p.diag)
 
     k_ref[...] = dot6(m[...], lt[...], NT)
 

time: 114 us -> 114 us (level)
  no operation moved by 1% of the time
where the time goes in v5:
time: 114 us
  Pallas kernels  112 us (98%)
  local copies, waits for them, and re-layouts  1.32 us (1%)
    pallas_call x1, Pallas kernels, panel_call(): pl.pallas_call(panel_kernel, out_shape=jax.ShapeDtypeStruct((NY, W, W), F...  112 us

profile of v5, /device:TPU:66, one launch (start us, length us, event | category | flops | bytes accessed | tf_op | source)
XLA Modules:
  0.0 113.7 jit_solution(13653128191026508259)
XLA Ops:
  0.0 112.4 %panel_step.1 = f32[8,256,256]{2,1,0:T(8,128)S(1)} custom-call(f32[8,256,256]{2,1,0:T(8,128)} %bitcast.5), custom_call_target="tpu_custom_call" | custom-call | tf_op jit(solution)/shard_map/panel_step/pallas_call | solution.py:887
  112.4 1.3 %copy.4 = f32[8,1,256,256]{3,2,1,0:T(8,128)} copy(f32[8,1,256,256]{3,2,1,0:T(8,128)S(1)} %bitcast.4) | data formatting | bytes 4194304
